TPU v7x, 32 devices: a whole 2x2x4 slice. The times are simulated.
32 devices in a mesh: row: 2 (over core), col: 16 (over z, y, x).
Axes of the slice: x: 2, y: 2, z: 4, core: 2. Of those that a mesh axis runs over, the one named last changes fastest.
Arguments:
- pair: bfloat16 [192, 192, 128], P('row', 'col'), may hold values from -6 to 6
- seq: bfloat16 [192, 1024], P(None, 'col'), may hold values from -6 to 6
- w_hidden: bfloat16 [128, 512], replicated, may hold values from -0.5 to 0.5
- w_back: bfloat16 [512, 128], replicated, may hold values from -0.25 to 0.25
- w_bias: bfloat16 [128, 32], replicated, may hold values from -0.5 to 0.5
- w_query: bfloat16 [1024, 1024], replicated, may hold values from -10 to 10
- w_key: bfloat16 [1024, 1024], replicated, may hold values from -0.1875 to 0.1875
- w_value: bfloat16 [1024, 1024], replicated, may hold values from -0.1875 to 0.1875
- w_out: bfloat16 [1024, 1024], replicated, may hold values from -0.1875 to 0.1875
- w_project: bfloat16 [1024, 128], replicated, may hold values from -0.1875 to 0.1875
- w_pair: bfloat16 [128, 128], replicated, may hold values from -0.5 to 0.5
Outputs:
- pair_out: bfloat16 [192, 192, 128], P('row', 'col')
- seq_new: bfloat16 [192, 1024], P('row', 'col')
All inputs are finite; a program needn't handle non-finite values.
Results may differ from a plain program's by a relative error of at most 0.013.
The roundings to bfloat16 on the way count: a program that leaves them out, or rounds other values in their place, can miss the bound.
Values may be sent and summed in bfloat16 or wider, within the bound.
No kernel may reach another device: no remote copies, remote signals or barrier semaphores. Data moves between devices by JAX's collectives and lax.ppermute only.
A program may use at most 128 MiB of HBM per device.

v0:
```python
import functools

import jax
import jax.numpy as jnp
from jax import lax
from jax.experimental import pallas as pl
from jax.experimental.pallas import tpu as pltpu
from jax.sharding import PartitionSpec as P

HEADS = 32
LANES = 128
eps_norm = 1e-05
f32 = jnp.float32
bf16 = jnp.bfloat16


def layer_norm(values_in):
    row_mean = jnp.mean(values_in, axis=-1, keepdims=True)
    centred = values_in - row_mean
    row_var = jnp.mean(centred * centred, axis=-1, keepdims=True)
    return centred * lax.rsqrt(row_var + eps_norm)


def dot(a, b):
    return jnp.dot(a, b, preferred_element_type=f32)


def dot_nt(a, b):
    return lax.dot_general(a, b, (((1,), (1,)), ((), ())), preferred_element_type=f32)


def round_up(n, m):
    return -(-n // m) * m


def one_hot_rows(shape, target):
    rows = lax.broadcasted_iota(jnp.int32, shape, 0)
    cols = lax.broadcasted_iota(jnp.int32, shape, 1)
    return (cols == target(rows)).astype(f32).astype(bf16)


def call(kernel, outs, args, scratch=(), flops=1000):
    vmem = pl.BlockSpec(memory_space=pltpu.VMEM)
    size = sum(round_up(a.size * a.dtype.itemsize, 4096) for a in args)
    size += sum(a.size * a.dtype.itemsize for a in outs)
    return pl.pallas_call(
        kernel,
        out_shape=outs,
        in_specs=[vmem] * len(args),
        out_specs=tuple(vmem for _ in outs),
        scratch_shapes=list(scratch),
        compiler_params=pltpu.CompilerParams(vmem_limit_bytes=56 * 1024 * 1024),
        cost_estimate=pl.CostEstimate(flops=flops, bytes_accessed=size, transcendentals=0),
    )(*args)


def pack_seq(n_row, rows, seq_ref, out_ref):
    feats = seq_ref.shape[0]
    fold = LANES // feats
    short = rows // fold
    row = lax.axis_index("row")
    for v in range(n_row):

        @pl.when(row == v)
        def _():
            parts = [
                seq_ref[:, v * rows + p * short : v * rows + (p + 1) * short].astype(f32)
                for p in range(fold)
            ]
            tile = jnp.concatenate(parts, axis=0).T.astype(bf16)
            out_ref[...] = jnp.broadcast_to(tile[None], out_ref.shape)


def bias_plan(rows, cols, n_col):
    own = rows // n_col
    keys = round_up(cols, 16)
    per_tile = LANES // HEADS
    full, rest = divmod(own, per_tile)
    split = per_tile // rest if rest and per_tile % rest == 0 else 1
    if rest and (keys // split) % 8:
        split = 1
    height = full * keys + (keys // split if rest else 0)
    return own, keys, full, rest, split, height


def transition(n_col, chunk, pair_ref, hidden_ref, back_ref, bias_ref, mid_ref, msg_ref, norm_ref):
    cols, rows, chans = pair_ref.shape
    own, keys, full, rest, split, _ = bias_plan(rows, cols, n_col)
    per_tile = LANES // HEADS
    if keys > cols:
        norm_ref[cols * rows :, :] = jnp.zeros(((keys - cols) * rows, chans), f32)

    def step(t):
        at = t * chunk
        pair = pair_ref[pl.ds(at, chunk)].reshape(chunk * rows, chans).astype(f32)
        normed = layer_norm(pair).astype(bf16)
        hidden = jnp.maximum(dot(normed, hidden_ref[...]), 0.0).astype(bf16)
        mid = (pair + dot(hidden, back_ref[...])).astype(bf16)
        mid_ref[pl.ds(at, chunk)] = mid.reshape(chunk, rows, chans)
        start = at * rows if isinstance(at, int) else pl.multiple_of(at * rows, 8)
        norm_ref[pl.ds(start, chunk * rows), :] = layer_norm(mid.astype(f32))

    if cols // chunk <= 4:
        for t in range(cols // chunk):
            step(t)
    else:
        pl.loop(0, cols // chunk)(step)

    w_t = bias_ref[...]
    zero = jnp.zeros_like(w_t)
    placed = [
        jnp.concatenate([w_t if k == p else zero for k in range(per_tile)], axis=0)
        for p in range(per_tile)
    ]

    def queries(q):
        parts = [norm_ref[pl.ds(c * own + q, keys, stride=rows), :] for c in range(n_col)]
        return jnp.concatenate(parts, axis=0)

    for tile in range(full):
        wide = jnp.concatenate(
            [queries(tile * per_tile + p).astype(bf16) for p in range(per_tile)], axis=1
        )
        acc = dot_nt(wide, jnp.concatenate(placed, axis=1))
        msg_ref[:, tile * keys : (tile + 1) * keys, :] = acc.reshape(n_col, keys, LANES)
    if rest:
        small = keys // split
        lhs, rhs = [], []
        for p in range(rest):
            q_rows = queries(full * per_tile + p).reshape(n_col, split, small, chans)
            for s in range(split):
                lhs.append(q_rows[:, s].reshape(n_col * small, chans).astype(bf16))
                rhs.append(placed[s * rest + p])
        acc = dot_nt(jnp.concatenate(lhs, axis=1), jnp.concatenate(rhs, axis=1))
        msg_ref[:, full * keys :, :] = acc.reshape(n_col, small, LANES)


def project_qkv(n_row, rows, own, *refs):
    n_in = 2 if n_row == 2 else 1
    seq_refs = refs[:n_in]
    wq_ref, wk_ref, wv_ref, k_ref, v_ref, qm_ref, own_ref, x_ref, xn_ref = refs[n_in:]
    n_col, short, _ = seq_refs[0].shape[-3:]
    width = x_ref.shape[1]
    feats = width // n_col
    fold = LANES // feats
    head_dim = width // HEADS
    length = x_ref.shape[0]
    row, col = lax.axis_index("row"), lax.axis_index("col")
    slot = lax.broadcasted_iota(jnp.int32, (short, LANES), 1) // feats

    def place(read, v):
        for g in range(width // LANES):
            got = [read(fold * g + s).astype(f32) for s in range(fold)]
            for p in range(fold):
                piece = got[p]
                for s in range(fold):
                    if s != p:
                        piece = jnp.where(
                            slot == s, pltpu.roll(got[s], (s - p) % fold * feats, 1), piece
                        )
                start = v * rows + p * short
                if not isinstance(start, int):
                    start = pl.multiple_of(start, 16)
                x_ref[pl.ds(start, short), g * LANES : (g + 1) * LANES] = piece

    if n_row == 2:
        place(lambda c: seq_refs[0][c], row)
        place(lambda c: seq_refs[1][c], 1 - row)
    else:
        pl.loop(0, n_row)(lambda v: place(lambda c: seq_refs[0][v, c], v))

    block = rows * (2 if n_row == 2 else 1)

    def step(b):
        start = b * block if isinstance(b, int) else pl.multiple_of(b * block, 16)
        at = pl.ds(start, block)
        normed = layer_norm(x_ref[at, :]).astype(bf16)
        xn_ref[at, :] = normed
        k_ref[at, :] = dot(normed, wk_ref[...]).astype(bf16)
        v_ref[at, :] = dot(normed, wv_ref[...]).astype(bf16)

    if length == block:
        step(0)
    else:
        pl.loop(0, length // block)(step)

    padded = own_ref.shape[0]
    pick = one_hot_rows((padded, length), lambda i: row * rows + col * own + i)
    own_ref[...] = dot(pick, x_ref[...].astype(bf16))
    queries = dot(dot(pick, xn_ref[...]).astype(bf16), wq_ref[...]).astype(bf16)
    spread = one_hot_rows((padded * HEADS, padded), lambda ih: ih // HEADS)
    wide = dot(spread, queries)
    head_of_row = lax.broadcasted_iota(jnp.int32, wide.shape, 0) % HEADS
    head_of_lane = lax.broadcasted_iota(jnp.int32, wide.shape, 1) // head_dim
    qm_ref[...] = jnp.where(head_of_row == head_of_lane, wide, 0.0).astype(bf16)


def attend(plan, cols, fold, msg_ref, k_ref, v_ref, qm_ref, own_ref, wo_ref, wp_ref, out_ref, bias_ref):
    own, keys, full, rest, split, _ = plan
    n_col = msg_ref.shape[0]
    length, width = k_ref.shape
    head_dim = width // HEADS
    padded = own_ref.shape[0]
    small = keys // split
    for c in range(n_col):
        for tile in range(full):
            bias_ref[c * cols : (c + 1) * cols, tile * LANES : (tile + 1) * LANES] = msg_ref[
                c, tile * keys : tile * keys + cols, :
            ]
        if rest:
            last = msg_ref[c, full * keys :, :]
            for s in range(split):
                height = min(small, cols - s * small)
                if height <= 0:
                    continue
                moved = last
                if s:
                    moved = pltpu.roll(last, LANES - s * rest * HEADS, 1)
                bias_ref[c * cols + s * small : c * cols + s * small + height, full * LANES :] = (
                    moved[:height]
                )
    scores = dot_nt(k_ref[...], qm_ref[...]) * head_dim ** (-0.5) + bias_ref[...]
    top = jnp.max(scores, axis=0, keepdims=True)
    weights = jnp.exp(scores - top)
    denom = jnp.sum(weights, axis=0, keepdims=True)
    by_query = (weights / denom).T
    high = by_query.astype(bf16)
    low = (by_query - high.astype(f32)).astype(bf16)
    values = v_ref[...]
    mixed = dot(high, values) + dot(low, values)
    head_of_row = lax.broadcasted_iota(jnp.int32, mixed.shape, 0) % HEADS
    head_of_lane = lax.broadcasted_iota(jnp.int32, mixed.shape, 1) // head_dim
    mixed = jnp.where(head_of_row == head_of_lane, mixed, 0.0)
    attended = jnp.sum(mixed.reshape(padded, HEADS, width), axis=1).astype(bf16)
    seq_next = (own_ref[...] + dot(attended, wo_ref[...])).astype(bf16)
    seq_wide = seq_next.astype(f32)
    projected = dot(layer_norm(seq_wide).astype(bf16), wp_ref[...]).astype(bf16).astype(f32)
    n_row = out_ref.shape[0]
    for g in range(width // LANES):
        tile = jnp.concatenate([projected, seq_wide[:, g * LANES : (g + 1) * LANES]], axis=0)
        out_ref[:, fold * g : fold * (g + 1)] = jnp.broadcast_to(
            tile.astype(bf16)[None, None], (n_row, fold) + tile.shape
        )


def update_pair(own, fold, msg_ref, mid_ref, wpair_ref, pair_ref, seq_ref, left_ref, slab_ref):
    cols, rows, chans = mid_ref.shape
    n_row, n_col, twice, _ = msg_ref.shape
    padded = twice // 2
    half = chans // 2
    row, col = lax.axis_index("row"), lax.axis_index("col")
    for c in range(n_col):
        block = msg_ref[row, c].astype(f32)
        left_ref[c * own : (c + 1) * own, :] = block[:own]
        slab_ref[c * own : (c + 1) * own, :] = block[padded : padded + own]
    feats = LANES // fold
    turned = slab_ref[...].T
    for s in range(fold):

        @pl.when(lax.rem(col, fold) == s)
        def _():
            seq_ref[...] = turned[s * feats : (s + 1) * feats].astype(bf16)

    both = left_ref[...]
    is_first = lax.broadcasted_iota(jnp.int32, (1, chans), 1) < half
    left = jnp.where(is_first, both, pltpu.roll(both, half, 1))
    blocks_each = cols // own
    first = col * blocks_each

    def step(t):
        at = first + t
        theirs = msg_ref[at // n_col, lax.rem(at, n_col)].astype(f32)[:padded]
        right = jnp.where(is_first, pltpu.roll(theirs, half, 1), theirs)
        feature = []
        for i in range(own):
            r = right[i : i + 1]
            feature.append(jnp.where(is_first, left * r, left - r).astype(bf16))
        out = dot(jnp.concatenate(feature, axis=0), wpair_ref[...])
        here = pl.ds(t * own, own)
        mid = mid_ref[here].astype(f32)
        pair_ref[here] = (mid + out.reshape(own, rows, chans)).astype(bf16)

    if blocks_each <= 4:
        for t in range(blocks_each):
            step(t)
    else:
        pl.loop(0, blocks_each)(step)


def local(pair, seq, w_hidden, w_back, w_bias, w_query, w_key, w_value, w_out, w_project, w_pair):
    shape = jax.ShapeDtypeStruct
    rows, cols, chans = pair.shape
    length, feats = seq.shape
    width = w_query.shape[0]
    n_row, n_col = lax.axis_size("row"), lax.axis_size("col")
    fold = LANES // feats
    short = rows // fold
    plan = bias_plan(rows, cols, n_col)
    own, keys, full, rest, _, height = plan
    padded = round_up(own, 8)
    hidden_units = w_hidden.shape[1]

    (seq_msg,) = call(
        functools.partial(pack_seq, n_row, rows), (shape((n_col, short, LANES), bf16),), (seq.T,)
    )
    seq_rows = lax.all_to_all(seq_msg, "col", split_axis=0, concat_axis=0, tiled=True)
    if n_row == 2:
        seq_parts = (seq_rows, lax.ppermute(seq_rows, "row", [(0, 1), (1, 0)]))
    else:
        seq_parts = (lax.all_gather(seq_rows, "row"),)

    chunk = max(k for k in range(1, cols + 1) if cols % k == 0 and k * rows <= 576)
    pair_mid, bias_msg = call(
        functools.partial(transition, n_col, chunk),
        (shape((cols, rows, chans), bf16), shape((n_col, height, LANES), f32)),
        (pair.transpose(1, 0, 2), w_hidden, w_back, w_bias.T),
        [pltpu.VMEM((keys * rows, chans), f32)],
        flops=4 * rows * cols * chans * hidden_units,
    )
    bias_rows = lax.all_to_all(bias_msg, "col", split_axis=0, concat_axis=0, tiled=True)

    keys_proj, values_proj, queries, own_seq = call(
        functools.partial(project_qkv, n_row, rows, own),
        (
            shape((length, width), bf16),
            shape((length, width), bf16),
            shape((padded * HEADS, width), bf16),
            shape((padded, width), f32),
        ),
        seq_parts + (w_query, w_key, w_value),
        [pltpu.VMEM((length, width), f32), pltpu.VMEM((length, width), bf16)],
        flops=4 * length * width * width,
    )
    (out_msg,) = call(
        functools.partial(attend, plan, cols, fold),
        (shape((n_row, n_col, 2 * padded, LANES), bf16),),
        (bias_rows, keys_proj, values_proj, queries, own_seq, w_out, w_project),
        [pltpu.VMEM((length, padded * HEADS), f32)],
        flops=6 * length * padded * HEADS * width,
    )
    flat = out_msg.reshape(n_row * n_col, 2 * padded, LANES)
    got = lax.all_to_all(flat, ("row", "col"), split_axis=0, concat_axis=0, tiled=True)
    pair_out, seq_out = call(
        functools.partial(update_pair, own, fold),
        (shape((cols, rows, chans), bf16), shape((feats, rows), bf16)),
        (got.reshape(out_msg.shape), pair_mid, w_pair),
        [pltpu.VMEM((rows, LANES), f32), pltpu.VMEM((rows, LANES), f32)],
        flops=2 * rows * cols * chans * chans,
    )
    return (pair_out.transpose(1, 0, 2), seq_out.T)


def solution(mesh):
    return jax.shard_map(
        local,
        mesh=mesh,
        in_specs=(P("row", "col", None), P(None, "col")) + (P(),) * 9,
        out_specs=(P("row", "col", None), P("row", "col")),
        check_vma=False,
    )
```

profile of v0, /device:TPU:0, one launch (start us, length us, event | category | flops | bytes accessed | tf_op | source)
XLA Modules:
  0.0 52.0 jit_solution(1705500143352078767)
XLA Ops:
  0.6 1.6 %shard_map.123 = bf16[16,48,128]{2,1,0:T(8,128)(2,1)} custom-call(bf16[64,192]{1,0:T(8,128)(2,1)} %bitcast.9), custom_call_target="tpu_custom_call" | custom-call | flops 1000 | bytes 221184 | tf_op jit(solution)/shard_map/pallas_call | solution.py:46
  2.2 8.3 %all-to-all-start.1 = ((bf16[16,48,128]{2,1,0:T(8,128)(2,1)}), bf16[16,48,128]{2,1,0:T(8,128)(2,1)S(1)}, u32[]{:S(2)}, u32[]{:S(2)}) async-start(bf16[16,48,128]{2,1,0:T(8,128)(2,1)} %shard_map.123), calls=%async_computation.1 | async-start | bytes 393216 | tf_op jit(solution)/shard_map/all_to_all | solution.py:306
  10.5 3.5 %shard_map.122 = (bf16[12,96,128]{2,1,0:T(8,128)(2,1)}, f32[16,24,128]{2,1,0:T(8,128)}) custom-call(bf16[12,96,128]{2,1,0:T(8,128)(2,1)} %bitcast.10, bf16[128,512]{1,0:T(8,128)(2,1)} %hidden_ref.1, bf16[512,128]{1,0:T(8,128)(2,1)} %back_ref.1, bf16[32,128]{1,0:T(8,128)(2,1)} %bitcast.13), custom_call_target="tpu_custom_call" | custom-call | flops 301989888 | bytes 1056768 | tf_op jit(solution)/shard_map/pallas_call | solution.py:46
  14.1 5.2 %all-to-all-done.1.refs_0_ = bf16[16,48,128]{2,1,0:T(8,128)(2,1)S(1)} async-done(((bf16[16,48,128]{2,1,0:T(8,128)(2,1)}), bf16[16,48,128]{2,1,0:T(8,128)(2,1)S(1)}, u32[]{:S(2)}, u32[]{:S(2)}) %all-to-all-start.1) | async-done | bytes 196640 | tf_op jit(solution)/shard_map/all_to_all | solution.py:306
  19.2 0.0 copy-start
  19.2 3.5 %all-to-all-start = ((f32[16,24,128]{2,1,0:T(8,128)}), f32[16,24,128]{2,1,0:T(8,128)S(1)}, u32[]{:S(2)}, u32[]{:S(2)}) async-start(f32[16,24,128]{2,1,0:T(8,128)} %get-tuple-element.10), calls=%async_computation | async-start | bytes 393216 | tf_op jit(solution)/shard_map/all_to_all | solution.py:320
  22.8 0.1 collective-permute-start
  22.8 1.4 %collective-permute-done.refs_1_ = bf16[16,48,128]{2,1,0:T(8,128)(2,1)S(1)} collective-permute-done((bf16[16,48,128]{2,1,0:T(8,128)(2,1)S(1)}, bf16[16,48,128]{2,1,0:T(8,128)(2,1)S(1)}, u32[]{:S(2)}, u32[]{:S(2)}) %collective-permute-start) | collective-permute-done | bytes 196640 | tf_op jit(solution)/shard_map/ppermute | solution.py:308
  24.3 0.0 copy-done
  24.3 0.0 copy-start.2
  24.3 0.7 %copy-done.2 = bf16[16,48,128]{2,1,0:T(8,128)(2,1)} copy-done((bf16[16,48,128]{2,1,0:T(8,128)(2,1)}, bf16[16,48,128]{2,1,0:T(8,128)(2,1)S(1)}, u32[]{:S(2)}) %copy-start.2) | copy-done | bytes 196632
  24.9 5.8 %shard_map.124 = (bf16[192,1024]{1,0:T(8,128)(2,1)}, bf16[192,1024]{1,0:T(8,128)(2,1)}, bf16[256,1024]{1,0:T(8,128)(2,1)}, f32[8,1024]{1,0:T(8,128)}) custom-call(bf16[16,48,128]{2,1,0:T(8,128)(2,1)} %copy-done, bf16[16,48,128]{2,1,0:T(8,128)(2,1)} %copy-done.2, bf16[1024,1024]{1,0:T(8,128)(2,1)} %refs_2_.1, bf16[1024,1024]{1,0:T(8,128)(2,1)} %refs_3_.1, ...), custom_call_target="tpu_custom_call" | custom-call | flops 805306368 | bytes 8028160 | tf_op jit(solution)/shard_map/pallas_call | solution.py:46
  30.8 0.1 all-to-all-done.msg_ref
  30.8 0.0 copy-start.1
  30.8 0.7 %copy-done.1 = f32[16,24,128]{2,1,0:T(8,128)} copy-done((f32[16,24,128]{2,1,0:T(8,128)}, f32[16,24,128]{2,1,0:T(8,128)S(1)}, u32[]{:S(2)}) %copy-start.1) | copy-done | bytes 196632
  31.5 4.7 %shard_map.125 = bf16[2,16,16,128]{3,2,1,0:T(8,128)(2,1)} custom-call(f32[16,24,128]{2,1,0:T(8,128)} %copy-done.1, bf16[192,1024]{1,0:T(8,128)(2,1)} %get-tuple-element.11.k_ref, bf16[192,1024]{1,0:T(8,128)(2,1)} %get-tuple-element.12.v_ref, bf16[256,1024]{1,0:T(8,128)(2,1)} %get-tuple-element.13.qm_ref, f32[8,1024]{1,0:T(8,128)} %get-tuple-element.14.own_ref, ...), custom_call_target="tpu_custom_call" | custom-call | flops 301989888 | bytes 4030464 | tf_op jit(solution)/shard_map/pallas_call | solution.py:46
  36.1 13.8 %all_to_all.15 = bf16[32,16,128]{2,1,0:T(8,128)(2,1)} all-to-all(bf16[32,16,128]{2,1,0:T(8,128)(2,1)} %bitcast.7), channel_id=1, replica_groups=mesh['row'=2,'col'=16] {'row','col'}, dimensions={0} | all-to-all | bytes 262144 | tf_op jit(solution)/shard_map/all_to_all | solution.py:342
  49.9 2.1 %shard_map.126 = (bf16[12,96,128]{2,1,0:T(8,128)(2,1)}, bf16[64,96]{1,0:T(8,128)(2,1)}) custom-call(bf16[2,16,16,128]{3,2,1,0:T(8,128)(2,1)} %bitcast.8, bf16[12,96,128]{2,1,0:T(8,128)(2,1)} %get-tuple-element.15.mid_ref, bf16[128,128]{1,0:T(8,128)(2,1)} %wpair_ref.1), custom_call_target="tpu_custom_call" | custom-call | flops 37748736 | bytes 765952 | tf_op jit(solution)/shard_map/pallas_call | solution.py:46
Async XLA Ops:
  2.2 17.0 %all-to-all-start.1 = ((bf16[16,48,128]{2,1,0:T(8,128)(2,1)}), bf16[16,48,128]{2,1,0:T(8,128)(2,1)S(1)}, u32[]{:S(2)}, u32[]{:S(2)}) async-start(bf16[16,48,128]{2,1,0:T(8,128)(2,1)} %shard_map.123), calls=%async_computation.1 | async-start | bytes 393216 | tf_op jit(solution)/shard_map/all_to_all | solution.py:306
  19.2 5.0 %copy-start = (bf16[16,48,128]{2,1,0:T(8,128)(2,1)}, bf16[16,48,128]{2,1,0:T(8,128)(2,1)S(1)}, u32[]{:S(2)}) copy-start(bf16[16,48,128]{2,1,0:T(8,128)(2,1)S(1)} %all-to-all-done.1.refs_0_) | copy-start | bytes 589828
  19.2 11.6 %all-to-all-start = ((f32[16,24,128]{2,1,0:T(8,128)}), f32[16,24,128]{2,1,0:T(8,128)S(1)}, u32[]{:S(2)}, u32[]{:S(2)}) async-start(f32[16,24,128]{2,1,0:T(8,128)} %get-tuple-element.10), calls=%async_computation | async-start | bytes 393216 | tf_op jit(solution)/shard_map/all_to_all | solution.py:320
  22.8 1.5 %collective-permute-start = (bf16[16,48,128]{2,1,0:T(8,128)(2,1)S(1)}, bf16[16,48,128]{2,1,0:T(8,128)(2,1)S(1)}, u32[]{:S(2)}, u32[]{:S(2)}) collective-permute-start(bf16[16,48,128]{2,1,0:T(8,128)(2,1)S(1)} %all-to-all-done.1.refs_0_), channel_id=1, source_target_pairs={{0,16},{16,0},{1,17},{17,1},{2,18},{18,2},{3,19},{19,3},{4,20},{20... | collective-permute-start | bytes 589832 | tf_op jit(solution)/shard_map/ppermute | solution.py:308
  24.3 0.7 %copy-start.2 = (bf16[16,48,128]{2,1,0:T(8,128)(2,1)}, bf16[16,48,128]{2,1,0:T(8,128)(2,1)S(1)}, u32[]{:S(2)}) copy-start(bf16[16,48,128]{2,1,0:T(8,128)(2,1)S(1)} %collective-permute-done.refs_1_) | copy-start | bytes 589828
  30.8 0.7 %copy-start.1 = (f32[16,24,128]{2,1,0:T(8,128)}, f32[16,24,128]{2,1,0:T(8,128)S(1)}, u32[]{:S(2)}) copy-start(f32[16,24,128]{2,1,0:T(8,128)S(1)} %all-to-all-done.msg_ref) | copy-start | bytes 589828
where the time goes:
time: 52.5 us; the launch traced here: 52 us
  Pallas kernels  17.7 us (34%)
  blocking collectives  13.8 us (26%)
  starting transfers between devices  11.9 us (23%)
  waiting for transfers between devices  6.64 us (13%)
  local copies, waits for them, and re-layouts  1.36 us (3%)
  between operations  0.66 us (1%)
    pallas_call x5, Pallas kernels, call(): pl.pallas_call(kernel, out_shape=outs, in_specs=[vmem] * len(args), out_s...  17.7 us
    all_to_all x1, blocking collectives, local(): lax.all_to_all(flat, ('row', 'col'), split_axis=0, concat_axis=0, tiled=T...  13.8 us
    all_to_all x1, starting transfers between devices, local(): lax.all_to_all(seq_msg, 'col', split_axis=0, concat_axis=0, tiled=True)  8.31 us
    all_to_all x1, waiting for transfers between devices, local(): lax.all_to_all(seq_msg, 'col', split_axis=0, concat_axis=0, tiled=True)  5.16 us
    all_to_all x1, starting transfers between devices, local(): lax.all_to_all(bias_msg, 'col', split_axis=0, concat_axis=0, tiled=True)  3.52 us
    ppermute x1, waiting for transfers between devices, local(): seq_parts = (seq_rows, lax.ppermute(seq_rows, 'row', [(0, 1), (1, 0)]))  1.43 us
    unnamed x6, local copies, waits for them, and re-layouts  1.36 us
  transfers between devices with their start and end apart: 3, of which 3 were waited for; matrix products, arithmetic and copies ran while one was open for 0% of the time, Pallas kernels for 18%

commit v1 on v0

--- a/solution.py
+++ b/solution.py
@@ -1,4 +1,5 @@
 import functools
+import math
 
 import jax
 import jax.numpy as jnp
@@ -39,22 +40,31 @@
     return (cols == target(rows)).astype(f32).astype(bf16)
 
 
-def call(kernel, outs, args, scratch=(), flops=1000):
-    vmem = pl.BlockSpec(memory_space=pltpu.VMEM)
-    size = sum(round_up(a.size * a.dtype.itemsize, 4096) for a in args)
-    size += sum(a.size * a.dtype.itemsize for a in outs)
+def call(kernel, outs, args, scratch=(), flops=1000, room=16):
+    size = sum(a.size * a.dtype.itemsize for a, _ in args)
+    size += sum(math.prod(a.shape) * jnp.dtype(a.dtype).itemsize for a in outs)
+    space = {"V": pltpu.VMEM, "H": pltpu.HBM}
     return pl.pallas_call(
         kernel,
         out_shape=outs,
-        in_specs=[vmem] * len(args),
-        out_specs=tuple(vmem for _ in outs),
+        in_specs=[pl.BlockSpec(memory_space=space[where]) for _, where in args],
+        out_specs=tuple(pl.BlockSpec(memory_space=pltpu.VMEM) for _ in outs),
         scratch_shapes=list(scratch),
-        compiler_params=pltpu.CompilerParams(vmem_limit_bytes=56 * 1024 * 1024),
+        compiler_params=pltpu.CompilerParams(vmem_limit_bytes=room * 1024 * 1024),
         cost_estimate=pl.CostEstimate(flops=flops, bytes_accessed=size, transcendentals=0),
-    )(*args)
-
-
-def pack_seq(n_row, rows, seq_ref, out_ref):
+    )(*[pltpu.with_memory_space_constraint(a, space[where]) for a, where in args])
+
+
+def copies(sources, targets, sems):
+    started = [
+        pltpu.make_async_copy(s, t, sems.at[k]) for k, (s, t) in enumerate(zip(sources, targets))
+    ]
+    for one in started:
+        one.start()
+    return lambda k: started[k].wait()
+
+
+def pack_seq(n_row, rows, seq_ref, msg_ref):
     feats = seq_ref.shape[0]
     fold = LANES // feats
     short = rows // fold
@@ -68,7 +78,7 @@
                 for p in range(fold)
             ]
             tile = jnp.concatenate(parts, axis=0).T.astype(bf16)
-            out_ref[...] = jnp.broadcast_to(tile[None], out_ref.shape)
+            msg_ref[:, :short, :] = jnp.broadcast_to(tile[None], (msg_ref.shape[0],) + tile.shape)
 
 
 def bias_plan(rows, cols, n_col):
@@ -83,8 +93,15 @@
     return own, keys, full, rest, split, height
 
 
-def transition(n_col, chunk, pair_ref, hidden_ref, back_ref, bias_ref, mid_ref, msg_ref, norm_ref):
+def prepare(n_row, n_col, chunk, *refs):
+    mid_ref, msg_ref, seq_ref, hidden_ref, back_ref, bias_ref, pair_ref, norm_ref, sems = refs[5:]
+    wait = copies(refs[:5], (seq_ref, hidden_ref, back_ref, bias_ref, pair_ref), sems)
     cols, rows, chans = pair_ref.shape
+    short = rows * seq_ref.shape[0] // LANES
+    wait(0)
+    pack_seq(n_row, rows, seq_ref, msg_ref)
+    for k in range(1, 5):
+        wait(k)
     own, keys, full, rest, split, _ = bias_plan(rows, cols, n_col)
     per_tile = LANES // HEADS
     if keys > cols:
@@ -122,7 +139,8 @@
             [queries(tile * per_tile + p).astype(bf16) for p in range(per_tile)], axis=1
         )
         acc = dot_nt(wide, jnp.concatenate(placed, axis=1))
-        msg_ref[:, tile * keys : (tile + 1) * keys, :] = acc.reshape(n_col, keys, LANES)
+        at = short + tile * keys
+        msg_ref[:, at : at + keys, :] = acc.reshape(n_col, keys, LANES).astype(bf16)
     if rest:
         small = keys // split
         lhs, rhs = [], []
@@ -132,19 +150,25 @@
                 lhs.append(q_rows[:, s].reshape(n_col * small, chans).astype(bf16))
                 rhs.append(placed[s * rest + p])
         acc = dot_nt(jnp.concatenate(lhs, axis=1), jnp.concatenate(rhs, axis=1))
-        msg_ref[:, full * keys :, :] = acc.reshape(n_col, small, LANES)
-
-
-def project_qkv(n_row, rows, own, *refs):
+        msg_ref[:, short + full * keys :, :] = acc.reshape(n_col, small, LANES).astype(bf16)
+
+
+def attend(n_row, plan, rows, cols, *refs):
+    own, keys, full, rest, split, _ = plan
     n_in = 2 if n_row == 2 else 1
     seq_refs = refs[:n_in]
-    wq_ref, wk_ref, wv_ref, k_ref, v_ref, qm_ref, own_ref, x_ref, xn_ref = refs[n_in:]
-    n_col, short, _ = seq_refs[0].shape[-3:]
-    width = x_ref.shape[1]
+    wk_ref, *hbm_refs = refs[n_in : n_in + 5]
+    out_ref, wq_ref, wv_ref, wo_ref, wp_ref, x_ref, xn_ref, k_ref, v_ref, bias_ref, sems = refs[
+        n_in + 5 :
+    ]
+    wait = copies(hbm_refs, (wq_ref, wv_ref, wo_ref, wp_ref), sems)
+    n_col = seq_refs[0].shape[-3]
+    length, width = x_ref.shape
     feats = width // n_col
     fold = LANES // feats
+    short = rows // fold
     head_dim = width // HEADS
-    length = x_ref.shape[0]
+    padded = round_up(own, 8)
     row, col = lax.axis_index("row"), lax.axis_index("col")
     slot = lax.broadcasted_iota(jnp.int32, (short, LANES), 1) // feats
 
@@ -158,57 +182,55 @@
                         piece = jnp.where(
                             slot == s, pltpu.roll(got[s], (s - p) % fold * feats, 1), piece
                         )
-                start = v * rows + p * short
-                if not isinstance(start, int):
-                    start = pl.multiple_of(start, 16)
+                start = pl.multiple_of(v * rows + p * short, 16)
                 x_ref[pl.ds(start, short), g * LANES : (g + 1) * LANES] = piece
 
     if n_row == 2:
-        place(lambda c: seq_refs[0][c], row)
-        place(lambda c: seq_refs[1][c], 1 - row)
+        place(lambda c: seq_refs[0][c, :short, :], row)
+        place(lambda c: seq_refs[1][c, :short, :], 1 - row)
+        bias_of = lambda c, at, size: seq_refs[0][c, short + at : short + at + size, :]
     else:
-        pl.loop(0, n_row)(lambda v: place(lambda c: seq_refs[0][v, c], v))
+        pl.loop(0, n_row)(lambda v: place(lambda c: seq_refs[0][v, c, :short, :], v))
+        bias_of = lambda c, at, size: seq_refs[0][row, c, short + at : short + at + size, :]
 
     block = rows * (2 if n_row == 2 else 1)
 
-    def step(b):
-        start = b * block if isinstance(b, int) else pl.multiple_of(b * block, 16)
-        at = pl.ds(start, block)
+    def over_blocks(step):
+        if length == block:
+            step(pl.ds(0, block))
+        else:
+            pl.loop(0, length // block)(lambda b: step(pl.ds(pl.multiple_of(b * block, 16), block)))
+
+    def norm_and_keys(at):
         normed = layer_norm(x_ref[at, :]).astype(bf16)
         xn_ref[at, :] = normed
         k_ref[at, :] = dot(normed, wk_ref[...]).astype(bf16)
-        v_ref[at, :] = dot(normed, wv_ref[...]).astype(bf16)
-
-    if length == block:
-        step(0)
-    else:
-        pl.loop(0, length // block)(step)
-
-    padded = own_ref.shape[0]
+
+    def values(at):
+        v_ref[at, :] = dot(xn_ref[at, :], wv_ref[...]).astype(bf16)
+
+    over_blocks(norm_and_keys)
+
     pick = one_hot_rows((padded, length), lambda i: row * rows + col * own + i)
-    own_ref[...] = dot(pick, x_ref[...].astype(bf16))
-    queries = dot(dot(pick, xn_ref[...]).astype(bf16), wq_ref[...]).astype(bf16)
+    own_seq = dot(pick, x_ref[...].astype(bf16))
+    own_norm = dot(pick, xn_ref[...]).astype(bf16)
+    wait(0)
+    queries = dot(own_norm, wq_ref[...]).astype(bf16)
     spread = one_hot_rows((padded * HEADS, padded), lambda ih: ih // HEADS)
     wide = dot(spread, queries)
     head_of_row = lax.broadcasted_iota(jnp.int32, wide.shape, 0) % HEADS
     head_of_lane = lax.broadcasted_iota(jnp.int32, wide.shape, 1) // head_dim
-    qm_ref[...] = jnp.where(head_of_row == head_of_lane, wide, 0.0).astype(bf16)
-
-
-def attend(plan, cols, fold, msg_ref, k_ref, v_ref, qm_ref, own_ref, wo_ref, wp_ref, out_ref, bias_ref):
-    own, keys, full, rest, split, _ = plan
-    n_col = msg_ref.shape[0]
-    length, width = k_ref.shape
-    head_dim = width // HEADS
-    padded = own_ref.shape[0]
+    same_head = head_of_row == head_of_lane
+    by_head = jnp.where(same_head, wide, 0.0).astype(bf16)
+
     small = keys // split
     for c in range(n_col):
         for tile in range(full):
-            bias_ref[c * cols : (c + 1) * cols, tile * LANES : (tile + 1) * LANES] = msg_ref[
-                c, tile * keys : tile * keys + cols, :
-            ]
+            bias_ref[c * cols : (c + 1) * cols, tile * LANES : (tile + 1) * LANES] = bias_of(
+                c, tile * keys, keys
+            ).astype(f32)[:cols]
         if rest:
-            last = msg_ref[c, full * keys :, :]
+            last = bias_of(c, full * keys, small).astype(f32)
             for s in range(split):
                 height = min(small, cols - s * small)
                 if height <= 0:
@@ -219,23 +241,23 @@
                 bias_ref[c * cols + s * small : c * cols + s * small + height, full * LANES :] = (
                     moved[:height]
                 )
-    scores = dot_nt(k_ref[...], qm_ref[...]) * head_dim ** (-0.5) + bias_ref[...]
+    scores = dot_nt(k_ref[...], by_head) * head_dim ** (-0.5) + bias_ref[...]
     top = jnp.max(scores, axis=0, keepdims=True)
     weights = jnp.exp(scores - top)
     denom = jnp.sum(weights, axis=0, keepdims=True)
     by_query = (weights / denom).T
     high = by_query.astype(bf16)
     low = (by_query - high.astype(f32)).astype(bf16)
-    values = v_ref[...]
-    mixed = dot(high, values) + dot(low, values)
-    head_of_row = lax.broadcasted_iota(jnp.int32, mixed.shape, 0) % HEADS
-    head_of_lane = lax.broadcasted_iota(jnp.int32, mixed.shape, 1) // head_dim
-    mixed = jnp.where(head_of_row == head_of_lane, mixed, 0.0)
+    wait(1)
+    over_blocks(values)
+    mixed = dot(high, v_ref[...]) + dot(low, v_ref[...])
+    mixed = jnp.where(same_head, mixed, 0.0)
     attended = jnp.sum(mixed.reshape(padded, HEADS, width), axis=1).astype(bf16)
-    seq_next = (own_ref[...] + dot(attended, wo_ref[...])).astype(bf16)
+    wait(2)
+    seq_next = (own_seq + dot(attended, wo_ref[...])).astype(bf16)
     seq_wide = seq_next.astype(f32)
+    wait(3)
     projected = dot(layer_norm(seq_wide).astype(bf16), wp_ref[...]).astype(bf16).astype(f32)
-    n_row = out_ref.shape[0]
     for g in range(width // LANES):
         tile = jnp.concatenate([projected, seq_wide[:, g * LANES : (g + 1) * LANES]], axis=0)
         out_ref[:, fold * g : fold * (g + 1)] = jnp.broadcast_to(
@@ -288,7 +310,7 @@
 
 
 def local(pair, seq, w_hidden, w_back, w_bias, w_query, w_key, w_value, w_out, w_project, w_pair):
-    shape = jax.ShapeDtypeStruct
+    shape = pltpu.VMEM
     rows, cols, chans = pair.shape
     length, feats = seq.shape
     width = w_query.shape[0]
@@ -300,50 +322,57 @@
     padded = round_up(own, 8)
     hidden_units = w_hidden.shape[1]
 
-    (seq_msg,) = call(
-        functools.partial(pack_seq, n_row, rows), (shape((n_col, short, LANES), bf16),), (seq.T,)
+    chunk = max(k for k in range(1, cols + 1) if cols % k == 0 and k * rows <= 576)
+    pair_mid, msg = call(
+        functools.partial(prepare, n_row, n_col, chunk),
+        (shape((cols, rows, chans), bf16), shape((n_col, short + height, LANES), bf16)),
+        [(a, "H") for a in (seq.T, w_hidden, w_back, w_bias.T, pair.transpose(1, 0, 2))],
+        [
+            shape((feats, length), bf16),
+            shape(w_hidden.shape, bf16),
+            shape(w_back.shape, bf16),
+            shape(w_bias.shape[::-1], bf16),
+            shape((cols, rows, chans), bf16),
+            shape((keys * rows, chans), f32),
+            pltpu.SemaphoreType.DMA((5,)),
+        ],
+        flops=4 * rows * cols * chans * hidden_units,
+        room=24,
     )
-    seq_rows = lax.all_to_all(seq_msg, "col", split_axis=0, concat_axis=0, tiled=True)
+    got = lax.all_to_all(msg, "col", split_axis=0, concat_axis=0, tiled=True)
     if n_row == 2:
-        seq_parts = (seq_rows, lax.ppermute(seq_rows, "row", [(0, 1), (1, 0)]))
+        parts = (got, lax.ppermute(got, "row", [(0, 1), (1, 0)]))
     else:
-        seq_parts = (lax.all_gather(seq_rows, "row"),)
-
-    chunk = max(k for k in range(1, cols + 1) if cols % k == 0 and k * rows <= 576)
-    pair_mid, bias_msg = call(
-        functools.partial(transition, n_col, chunk),
-        (shape((cols, rows, chans), bf16), shape((n_col, height, LANES), f32)),
-        (pair.transpose(1, 0, 2), w_hidden, w_back, w_bias.T),
-        [pltpu.VMEM((keys * rows, chans), f32)],
-        flops=4 * rows * cols * chans * hidden_units,
-    )
-    bias_rows = lax.all_to_all(bias_msg, "col", split_axis=0, concat_axis=0, tiled=True)
-
-    keys_proj, values_proj, queries, own_seq = call(
-        functools.partial(project_qkv, n_row, rows, own),
-        (
+        parts = (lax.all_gather(got, "row"),)
+    (out_msg,) = call(
+        functools.partial(attend, n_row, plan, rows, cols),
+        (shape((n_row, n_col, 2 * padded, LANES), bf16),),
+        [(a, "V") for a in parts + (w_key,)]
+        + [(a, "H") for a in (w_query, w_value, w_out, w_project)],
+        [
+            shape((width, width), bf16),
+            shape((width, width), bf16),
+            shape((width, width), bf16),
+            shape(w_project.shape, bf16),
+            shape((length, width), f32),
             shape((length, width), bf16),
             shape((length, width), bf16),
-            shape((padded * HEADS, width), bf16),
-            shape((padded, width), f32),
-        ),
-        seq_parts + (w_query, w_key, w_value),
-        [pltpu.VMEM((length, width), f32), pltpu.VMEM((length, width), bf16)],
-        flops=4 * length * width * width,
-    )
-    (out_msg,) = call(
-        functools.partial(attend, plan, cols, fold),
-        (shape((n_row, n_col, 2 * padded, LANES), bf16),),
-        (bias_rows, keys_proj, values_proj, queries, own_seq, w_out, w_project),
-        [pltpu.VMEM((length, padded * HEADS), f32)],
-        flops=6 * length * padded * HEADS * width,
+            shape((length, width), bf16),
+            shape((length, padded * HEADS), f32),
+            pltpu.SemaphoreType.DMA((4,)),
+        ],
+        flops=6 * length * width * width,
+        room=40,
     )
     flat = out_msg.reshape(n_row * n_col, 2 * padded, LANES)
     got = lax.all_to_all(flat, ("row", "col"), split_axis=0, concat_axis=0, tiled=True)
     pair_out, seq_out = call(
         functools.partial(update_pair, own, fold),
-        (shape((cols, rows, chans), bf16), shape((feats, rows), bf16)),
-        (got.reshape(out_msg.shape), pair_mid, w_pair),
+        (
+            jax.ShapeDtypeStruct((cols, rows, chans), bf16),
+            jax.ShapeDtypeStruct((feats, rows), bf16),
+        ),
+        [(a, "V") for a in (got.reshape(out_msg.shape), pair_mid, w_pair)],
         [pltpu.VMEM((rows, LANES), f32), pltpu.VMEM((rows, LANES), f32)],
         flops=2 * rows * cols * chans * chans,
     )

time: 52.5 us -> 42.6 us (0.81)
  blocking collectives: 13.8 us -> 28.9 us
  starting transfers between devices: 11.9 us -> 0.01 us
  Pallas kernels: 17.7 us -> 9.55 us
  waiting for transfers between devices: 6.64 us -> 1.58 us
    all_to_all x0 -> x1, blocking collectives: none -> 18.8 us  [local(): got = lax.all_to_all(msg, 'col', split_axis=0, concat_axis=0, tiled=True)]
    all_to_all x2 -> x0, starting transfers between devices: 11.8 us -> none  [the longest x1 8.31 us: local(): lax.all_to_all(seq_msg, 'col', split_axis=0, concat_axis=0, tiled=True)]
    pallas_call x5 -> x3, Pallas kernels: 17.7 us -> 9.55 us  [call(): pl.pallas_call(kernel, out_shape=outs, in_specs=[pl.BlockSpec(memory_spac...]
    all_to_all x2 -> x0, waiting for transfers between devices: 5.21 us -> none  [the longest x1 5.16 us: local(): lax.all_to_all(seq_msg, 'col', split_axis=0, concat_axis=0, tiled=True)]
    all_to_all x1, blocking collectives: 13.8 us -> 10.1 us  [local(): lax.all_to_all(flat, ('row', 'col'), split_axis=0, concat_axis=0, tiled=T...]
    unnamed x6 -> x4, local copies, waits for them, and re-layouts: 1.36 us -> 1.6 us
  transfers between devices with their start and end apart: 3 -> 1, of which waited for: 3 -> 1; matrix products, arithmetic and copies ran while one was open for 0% -> 0% of each run, Pallas kernels for 18% -> 0%
where the time goes in v1:
time: 42.6 us; the launch traced here: 42.3 us
  blocking collectives  28.9 us (68%)
  Pallas kernels  9.55 us (22%)
  local copies, waits for them, and re-layouts  1.6 us (4%)
  waiting for transfers between devices  1.58 us (4%)
  between operations  0.66 us (2%)
    all_to_all x1, blocking collectives, local(): got = lax.all_to_all(msg, 'col', split_axis=0, concat_axis=0, tiled=True)  18.8 us
    all_to_all x1, blocking collectives, local(): lax.all_to_all(flat, ('row', 'col'), split_axis=0, concat_axis=0, tiled=T...  10.1 us
    pallas_call x3, Pallas kernels, call(): pl.pallas_call(kernel, out_shape=outs, in_specs=[pl.BlockSpec(memory_spac...  9.55 us
    unnamed x4, local copies, waits for them, and re-layouts  1.6 us
    ppermute x1, waiting for transfers between devices, local(): parts = (got, lax.ppermute(got, 'row', [(0, 1), (1, 0)]))  1.58 us
  transfers between devices with their start and end apart: 1, of which 1 were waited for; matrix products, arithmetic and copies ran while one was open for 0% of the time, Pallas kernels for 0%

profile of v1, /device:TPU:0, one launch (start us, length us, event | category | flops | bytes accessed | tf_op | source)
XLA Modules:
  0.0 42.3 jit_solution(10608743052534885610)
XLA Ops:
  0.6 3.0 %shard_map.122 = (bf16[12,96,128]{2,1,0:T(8,128)(2,1)S(1)}, bf16[16,72,128]{2,1,0:T(8,128)(2,1)S(1)}) custom-call(bf16[64,192]{1,0:T(8,128)(2,1)} %bitcast.11, bf16[128,512]{1,0:T(8,128)(2,1)} %refs_1_.1, bf16[512,128]{1,0:T(8,128)(2,1)} %refs_2_.2, bf16[32,128]{1,0:T(8,128)(2,1)} %bitcast.13, bf16[12,96,128]{2,1,0:T(8,128)(2,1)} %bitcast.9), custom_call_target="tpu_custom_call" | custom-call | flops 301989888 | bytes 1179648 | tf_op jit(solution)/shard_map/pallas_call | solution.py:47
  3.6 0.0 copy-start.1
  3.6 18.8 %all_to_all.10.refs_0_ = bf16[16,72,128]{2,1,0:T(8,128)(2,1)S(1)} all-to-all(bf16[16,72,128]{2,1,0:T(8,128)(2,1)S(1)} %get-tuple-element.6), channel_id=1, replica_groups=mesh['row'=2,'col'=16] {'col'}, dimensions={0} | all-to-all | bytes 589824 | tf_op jit(solution)/shard_map/all_to_all | solution.py:342
  22.4 0.0 collective-permute-start
  22.4 1.6 %collective-permute-done.refs_1_ = bf16[16,72,128]{2,1,0:T(8,128)(2,1)S(1)} collective-permute-done((bf16[16,72,128]{2,1,0:T(8,128)(2,1)S(1)}, bf16[16,72,128]{2,1,0:T(8,128)(2,1)S(1)}, u32[]{:S(2)}, u32[]{:S(2)}) %collective-permute-start) | collective-permute-done | bytes 294944 | tf_op jit(solution)/shard_map/ppermute | solution.py:344
  24.0 0.0 copy-start
  24.0 1.6 %copy-done = bf16[1024,1024]{1,0:T(8,128)(2,1)S(1)} copy-done((bf16[1024,1024]{1,0:T(8,128)(2,1)S(1)}, bf16[1024,1024]{1,0:T(8,128)(2,1)}, u32[]{:S(2)}) %copy-start) | copy-done | bytes 2097176
  25.6 5.4 %shard_map.123 = bf16[2,16,16,128]{3,2,1,0:T(8,128)(2,1)S(1)} custom-call(bf16[16,72,128]{2,1,0:T(8,128)(2,1)S(1)} %all_to_all.10.refs_0_, bf16[16,72,128]{2,1,0:T(8,128)(2,1)S(1)} %collective-permute-done.refs_1_, bf16[1024,1024]{1,0:T(8,128)(2,1)S(1)} %copy-done, bf16[1024,1024]{1,0:T(8,128)(2,1)} %refs_3_.1, bf16[1024,1024]{1,0:T(8,128)(2,1)} %refs_4_.1, ...), custom_call_target="tpu_custom_call" | custom-call | flops 1207959552 | bytes 9371648 | tf_op jit(solution)/shard_map/pallas_call | solution.py:47
  31.0 10.1 %all_to_all.11 = bf16[32,16,128]{2,1,0:T(8,128)(2,1)S(1)} all-to-all(bf16[32,16,128]{2,1,0:T(8,128)(2,1)S(1)} %bitcast.7), channel_id=1, replica_groups=mesh['row'=2,'col'=16] {'row','col'}, dimensions={0} | all-to-all | bytes 262144 | tf_op jit(solution)/shard_map/all_to_all | solution.py:368
  41.2 0.0 copy-done.1
  41.2 1.1 %shard_map.124 = (bf16[12,96,128]{2,1,0:T(8,128)(2,1)}, bf16[64,96]{1,0:T(8,128)(2,1)}) custom-call(bf16[2,16,16,128]{3,2,1,0:T(8,128)(2,1)S(1)} %bitcast.8, bf16[12,96,128]{2,1,0:T(8,128)(2,1)S(1)} %get-tuple-element.7.mid_ref, bf16[128,128]{1,0:T(8,128)(2,1)S(1)} %copy-done.1), custom_call_target="tpu_custom_call" | custom-call | flops 37748736 | bytes 765952 | tf_op jit(solution)/shard_map/pallas_call | solution.py:47
Async XLA Ops:
  3.6 37.6 %copy-start.1 = (bf16[128,128]{1,0:T(8,128)(2,1)S(1)}, bf16[128,128]{1,0:T(8,128)(2,1)}, u32[]{:S(2)}) copy-start(bf16[128,128]{1,0:T(8,128)(2,1)} %wpair_ref.1) | copy-start | bytes 98308
  22.4 1.6 %collective-permute-start = (bf16[16,72,128]{2,1,0:T(8,128)(2,1)S(1)}, bf16[16,72,128]{2,1,0:T(8,128)(2,1)S(1)}, u32[]{:S(2)}, u32[]{:S(2)}) collective-permute-start(bf16[16,72,128]{2,1,0:T(8,128)(2,1)S(1)} %all_to_all.10.refs_0_), channel_id=1, source_target_pairs={{0,16},{16,0},{1,17},{17,1},{2,18},{18,2},{3,19},{19,3},{4,20},{20... | collective-permute-start | bytes 884744 | tf_op jit(solution)/shard_map/ppermute | solution.py:344
  24.0 1.6 %copy-start = (bf16[1024,1024]{1,0:T(8,128)(2,1)S(1)}, bf16[1024,1024]{1,0:T(8,128)(2,1)}, u32[]{:S(2)}) copy-start(bf16[1024,1024]{1,0:T(8,128)(2,1)} %refs_2_.3) | copy-start | bytes 6291460

commit v2 on v1

--- a/solution.py
+++ b/solution.py
@@ -64,6 +64,10 @@
     return lambda k: started[k].wait()
 
 
+def stage(body):
+    pl.when(lax.axis_index("row") >= 0)(body)
+
+
 def pack_seq(n_row, rows, seq_ref, msg_ref):
     feats = seq_ref.shape[0]
     fold = LANES // feats
@@ -94,14 +98,24 @@
 
 
 def prepare(n_row, n_col, chunk, *refs):
-    mid_ref, msg_ref, seq_ref, hidden_ref, back_ref, bias_ref, pair_ref, norm_ref, sems = refs[5:]
-    wait = copies(refs[:5], (seq_ref, hidden_ref, back_ref, bias_ref, pair_ref), sems)
+    mid_ref, msg_ref, wk_ref, seq_ref, hidden_ref, back_ref, bias_ref, pair_ref, norm_ref, sems = (
+        refs[6:]
+    )
+    wait = copies(refs[:6], (seq_ref, hidden_ref, back_ref, bias_ref, pair_ref, wk_ref), sems)
     cols, rows, chans = pair_ref.shape
     short = rows * seq_ref.shape[0] // LANES
     wait(0)
     pack_seq(n_row, rows, seq_ref, msg_ref)
     for k in range(1, 5):
         wait(k)
+    stage(lambda: transition(n_row, n_col, chunk, short, hidden_ref, back_ref, bias_ref, pair_ref, mid_ref, msg_ref, norm_ref))
+    wait(5)
+
+
+def transition(
+    n_row, n_col, chunk, short, hidden_ref, back_ref, bias_ref, pair_ref, mid_ref, msg_ref, norm_ref
+):
+    cols, rows, chans = pair_ref.shape
     own, keys, full, rest, split, _ = bias_plan(rows, cols, n_col)
     per_tile = LANES // HEADS
     if keys > cols:
@@ -153,116 +167,168 @@
         msg_ref[:, short + full * keys :, :] = acc.reshape(n_col, small, LANES).astype(bf16)
 
 
-def attend(n_row, plan, rows, cols, *refs):
+def place(read, feats, short, x_ref, start):
+    fold = LANES // feats
+    slot = lax.broadcasted_iota(jnp.int32, (short, LANES), 1) // feats
+    for g in range(x_ref.shape[1] // LANES):
+        got = [read(fold * g + s).astype(f32) for s in range(fold)]
+        for p in range(fold):
+            piece = got[p]
+            for s in range(fold):
+                if s != p:
+                    piece = jnp.where(
+                        slot == s, pltpu.roll(got[s], (s - p) % fold * feats, 1), piece
+                    )
+            at = pl.multiple_of(start + p * short, 16)
+            x_ref[pl.ds(at, short), g * LANES : (g + 1) * LANES] = piece
+
+
+def own_block(
+    plan, rows, cols,
+    got_ref, wk_ref, wq_hbm,
+    x_out, k_ref, by_head_ref, own_ref, bias_ref,
+    wq_ref, x_ref, raw_ref, norm_ref, sems,
+):
+    wait = copies((wq_hbm,), (wq_ref,), sems)
     own, keys, full, rest, split, _ = plan
-    n_in = 2 if n_row == 2 else 1
-    seq_refs = refs[:n_in]
-    wk_ref, *hbm_refs = refs[n_in : n_in + 5]
-    out_ref, wq_ref, wv_ref, wo_ref, wp_ref, x_ref, xn_ref, k_ref, v_ref, bias_ref, sems = refs[
-        n_in + 5 :
-    ]
-    wait = copies(hbm_refs, (wq_ref, wv_ref, wo_ref, wp_ref), sems)
-    n_col = seq_refs[0].shape[-3]
-    length, width = x_ref.shape
+    n_col = got_ref.shape[0]
+    width = x_ref.shape[1]
+    feats = width // n_col
+    short = rows * feats // LANES
+    head_dim = width // HEADS
+    padded = own_ref.shape[0]
+    col = lax.axis_index("col")
+    @stage
+    def _():
+        place(lambda c: got_ref[c, :short, :], feats, short, x_ref, 0)
+        normed = layer_norm(x_ref[...]).astype(bf16)
+        x_out[...] = normed
+        pick = one_hot_rows((padded, rows), lambda i: col * own + i)
+        own_ref[...] = dot(pick, x_ref[...].astype(bf16))
+        norm_ref[...] = dot(pick, normed).astype(bf16)
+        k_ref[...] = dot(normed, wk_ref[...]).astype(bf16)
+
+        small = keys // split
+        for c in range(n_col):
+            for tile in range(full):
+                at = short + tile * keys
+                raw_ref[c * cols : (c + 1) * cols, tile * LANES : (tile + 1) * LANES] = got_ref[
+                    c, at : at + keys, :
+                ].astype(f32)[:cols]
+            if rest:
+                last = got_ref[c, short + full * keys : short + full * keys + small, :].astype(f32)
+                for s in range(split):
+                    height = min(small, cols - s * small)
+                    if height <= 0:
+                        continue
+                    moved = last
+                    if s:
+                        moved = pltpu.roll(last, LANES - s * rest * HEADS, 1)
+                    raw_ref[c * cols + s * small : c * cols + s * small + height, full * LANES :] = (
+                        moved[:height]
+                    )
+        given = (raw_ref.shape[1], padded * HEADS)
+        source = lax.broadcasted_iota(jnp.int32, given, 0)
+        target = lax.broadcasted_iota(jnp.int32, given, 1)
+        query = target % padded
+        same = (source == query * HEADS + target // padded) & (query < own)
+        bias_ref[...] = dot(raw_ref[...].astype(bf16), same.astype(f32).astype(bf16))
+
+    wait(0)
+
+    @stage
+    def _():
+        queries = dot(norm_ref[...], wq_ref[...]).astype(bf16)
+        spread = one_hot_rows((padded * HEADS, padded), lambda hi: hi % padded)
+        wide = dot(spread, queries)
+        head_of_row = lax.broadcasted_iota(jnp.int32, wide.shape, 0) // padded
+        head_of_lane = lax.broadcasted_iota(jnp.int32, wide.shape, 1) // head_dim
+        by_head_ref[...] = jnp.where(head_of_row == head_of_lane, wide, 0.0).astype(bf16)
+
+
+def attend(
+    rows,
+    others_ref, x_own, k_own, by_head_ref, own_ref, bias_ref, wk_ref, wv_hbm, wo_hbm, wp_hbm,
+    out_ref,
+    wv_ref, wo_ref, wp_ref, x_ref, xn_ref, k_ref, v_ref, w_ref, att_ref, sems,
+):
+    wait = copies((wv_hbm, wo_hbm, wp_hbm), (wv_ref, wo_ref, wp_ref), sems)
+    n_col = others_ref.shape[-3]
+    n_row = out_ref.shape[0]
+    length, width = k_ref.shape
     feats = width // n_col
     fold = LANES // feats
     short = rows // fold
     head_dim = width // HEADS
-    padded = round_up(own, 8)
-    row, col = lax.axis_index("row"), lax.axis_index("col")
-    slot = lax.broadcasted_iota(jnp.int32, (short, LANES), 1) // feats
-
-    def place(read, v):
-        for g in range(width // LANES):
-            got = [read(fold * g + s).astype(f32) for s in range(fold)]
-            for p in range(fold):
-                piece = got[p]
-                for s in range(fold):
-                    if s != p:
-                        piece = jnp.where(
-                            slot == s, pltpu.roll(got[s], (s - p) % fold * feats, 1), piece
-                        )
-                start = pl.multiple_of(v * rows + p * short, 16)
-                x_ref[pl.ds(start, short), g * LANES : (g + 1) * LANES] = piece
-
-    if n_row == 2:
-        place(lambda c: seq_refs[0][c, :short, :], row)
-        place(lambda c: seq_refs[1][c, :short, :], 1 - row)
-        bias_of = lambda c, at, size: seq_refs[0][c, short + at : short + at + size, :]
-    else:
-        pl.loop(0, n_row)(lambda v: place(lambda c: seq_refs[0][v, c, :short, :], v))
-        bias_of = lambda c, at, size: seq_refs[0][row, c, short + at : short + at + size, :]
-
-    block = rows * (2 if n_row == 2 else 1)
-
-    def over_blocks(step):
-        if length == block:
-            step(pl.ds(0, block))
-        else:
-            pl.loop(0, length // block)(lambda b: step(pl.ds(pl.multiple_of(b * block, 16), block)))
-
-    def norm_and_keys(at):
-        normed = layer_norm(x_ref[at, :]).astype(bf16)
+    padded = own_ref.shape[0]
+    row = lax.axis_index("row")
+
+    def block(read, v):
+        place(read, feats, short, x_ref, 0)
+        normed = layer_norm(x_ref[...]).astype(bf16)
+        at = pl.ds(pl.multiple_of(v * rows, 16), rows)
         xn_ref[at, :] = normed
         k_ref[at, :] = dot(normed, wk_ref[...]).astype(bf16)
 
-    def values(at):
-        v_ref[at, :] = dot(xn_ref[at, :], wv_ref[...]).astype(bf16)
-
-    over_blocks(norm_and_keys)
-
-    pick = one_hot_rows((padded, length), lambda i: row * rows + col * own + i)
-    own_seq = dot(pick, x_ref[...].astype(bf16))
-    own_norm = dot(pick, xn_ref[...]).astype(bf16)
+    @stage
+    def _():
+        if n_row == 2:
+            block(lambda c: others_ref[c, :short, :], 1 - row)
+        else:
+            pl.loop(0, n_row)(lambda v: block(lambda c: others_ref[v, c, :short, :], v))
+        mine = pl.ds(pl.multiple_of(row * rows, 16), rows)
+        xn_ref[mine, :] = x_own[...]
+        k_ref[mine, :] = k_own[...]
+        scores = dot_nt(k_ref[...], by_head_ref[...]) * head_dim ** (-0.5) + bias_ref[...]
+        top = jnp.max(scores, axis=0, keepdims=True)
+        weights = jnp.exp(scores - top)
+        denom = jnp.sum(weights, axis=0, keepdims=True)
+        w_ref[...] = (weights / denom).T
+
     wait(0)
-    queries = dot(own_norm, wq_ref[...]).astype(bf16)
-    spread = one_hot_rows((padded * HEADS, padded), lambda ih: ih // HEADS)
-    wide = dot(spread, queries)
-    head_of_row = lax.broadcasted_iota(jnp.int32, wide.shape, 0) % HEADS
-    head_of_lane = lax.broadcasted_iota(jnp.int32, wide.shape, 1) // head_dim
-    same_head = head_of_row == head_of_lane
-    by_head = jnp.where(same_head, wide, 0.0).astype(bf16)
-
-    small = keys // split
-    for c in range(n_col):
-        for tile in range(full):
-            bias_ref[c * cols : (c + 1) * cols, tile * LANES : (tile + 1) * LANES] = bias_of(
-                c, tile * keys, keys
-            ).astype(f32)[:cols]
-        if rest:
-            last = bias_of(c, full * keys, small).astype(f32)
-            for s in range(split):
-                height = min(small, cols - s * small)
-                if height <= 0:
-                    continue
-                moved = last
-                if s:
-                    moved = pltpu.roll(last, LANES - s * rest * HEADS, 1)
-                bias_ref[c * cols + s * small : c * cols + s * small + height, full * LANES :] = (
-                    moved[:height]
-                )
-    scores = dot_nt(k_ref[...], by_head) * head_dim ** (-0.5) + bias_ref[...]
-    top = jnp.max(scores, axis=0, keepdims=True)
-    weights = jnp.exp(scores - top)
-    denom = jnp.sum(weights, axis=0, keepdims=True)
-    by_query = (weights / denom).T
-    high = by_query.astype(bf16)
-    low = (by_query - high.astype(f32)).astype(bf16)
+    step = rows * (2 if n_row == 2 else 1)
+    per_group = LANES // head_dim
+    tall = per_group * padded
+
+    @stage
+    def _():
+        if length == step:
+            v_ref[...] = dot(xn_ref[...], wv_ref[...]).astype(bf16)
+        else:
+
+            @pl.loop(0, length // step)
+            def _(b):
+                at = pl.ds(pl.multiple_of(b * step, 16), step)
+                v_ref[at, :] = dot(xn_ref[at, :], wv_ref[...]).astype(bf16)
+
+        lane_head = lax.broadcasted_iota(jnp.int32, (padded, LANES), 1) // head_dim
+        groups = []
+        for g in range(width // LANES):
+            weights = w_ref[g * tall : (g + 1) * tall, :]
+            high = weights.astype(bf16)
+            low = (weights - high.astype(f32)).astype(bf16)
+            both = jnp.concatenate([high, low], axis=0)
+            mixed = dot(both, v_ref[:, g * LANES : (g + 1) * LANES])
+            mixed = mixed[:tall] + mixed[tall:]
+            chosen = mixed[:padded]
+            for h in range(1, per_group):
+                chosen = jnp.where(lane_head == h, mixed[h * padded : (h + 1) * padded], chosen)
+            groups.append(chosen)
+        att_ref[...] = jnp.concatenate(groups, axis=1).astype(bf16)
+
     wait(1)
-    over_blocks(values)
-    mixed = dot(high, v_ref[...]) + dot(low, v_ref[...])
-    mixed = jnp.where(same_head, mixed, 0.0)
-    attended = jnp.sum(mixed.reshape(padded, HEADS, width), axis=1).astype(bf16)
     wait(2)
-    seq_next = (own_seq + dot(attended, wo_ref[...])).astype(bf16)
-    seq_wide = seq_next.astype(f32)
-    wait(3)
-    projected = dot(layer_norm(seq_wide).astype(bf16), wp_ref[...]).astype(bf16).astype(f32)
-    for g in range(width // LANES):
-        tile = jnp.concatenate([projected, seq_wide[:, g * LANES : (g + 1) * LANES]], axis=0)
-        out_ref[:, fold * g : fold * (g + 1)] = jnp.broadcast_to(
-            tile.astype(bf16)[None, None], (n_row, fold) + tile.shape
-        )
+
+    @stage
+    def _():
+        seq_next = (own_ref[...] + dot(att_ref[...], wo_ref[...])).astype(bf16)
+        seq_wide = seq_next.astype(f32)
+        projected = dot(layer_norm(seq_wide).astype(bf16), wp_ref[...]).astype(bf16).astype(f32)
+        for g in range(width // LANES):
+            tile = jnp.concatenate([projected, seq_wide[:, g * LANES : (g + 1) * LANES]], axis=0)
+            out_ref[:, fold * g : fold * (g + 1)] = jnp.broadcast_to(
+                tile.astype(bf16)[None, None], (n_row, fold) + tile.shape
+            )
 
 
 def update_pair(own, fold, msg_ref, mid_ref, wpair_ref, pair_ref, seq_ref, left_ref, slab_ref):
@@ -323,10 +389,14 @@
     hidden_units = w_hidden.shape[1]
 
     chunk = max(k for k in range(1, cols + 1) if cols % k == 0 and k * rows <= 576)
-    pair_mid, msg = call(
+    pair_mid, msg, wk = call(
         functools.partial(prepare, n_row, n_col, chunk),
-        (shape((cols, rows, chans), bf16), shape((n_col, short + height, LANES), bf16)),
-        [(a, "H") for a in (seq.T, w_hidden, w_back, w_bias.T, pair.transpose(1, 0, 2))],
+        (
+            shape((cols, rows, chans), bf16),
+            shape((n_col, short + height, LANES), bf16),
+            shape((width, width), bf16),
+        ),
+        [(a, "H") for a in (seq.T, w_hidden, w_back, w_bias.T, pair.transpose(1, 0, 2), w_key)],
         [
             shape((feats, length), bf16),
             shape(w_hidden.shape, bf16),
@@ -334,35 +404,56 @@
             shape(w_bias.shape[::-1], bf16),
             shape((cols, rows, chans), bf16),
             shape((keys * rows, chans), f32),
-            pltpu.SemaphoreType.DMA((5,)),
+            pltpu.SemaphoreType.DMA((6,)),
         ],
         flops=4 * rows * cols * chans * hidden_units,
         room=24,
     )
     got = lax.all_to_all(msg, "col", split_axis=0, concat_axis=0, tiled=True)
     if n_row == 2:
-        parts = (got, lax.ppermute(got, "row", [(0, 1), (1, 0)]))
+        others = lax.ppermute(got, "row", [(0, 1), (1, 0)])
     else:
-        parts = (lax.all_gather(got, "row"),)
+        others = lax.all_gather(got, "row")
+    tiles = full + (1 if rest else 0)
+    x_own, k_own, by_head, own_seq, bias = call(
+        functools.partial(own_block, plan, rows, cols),
+        (
+            shape((rows, width), bf16),
+            shape((rows, width), bf16),
+            shape((padded * HEADS, width), bf16),
+            shape((padded, width), f32),
+            shape((length, padded * HEADS), f32),
+        ),
+        [(got, "V"), (wk, "V"), (w_query, "H")],
+        [
+            shape((width, width), bf16),
+            shape((rows, width), f32),
+            shape((length, tiles * LANES), f32),
+            shape((padded, width), bf16),
+            pltpu.SemaphoreType.DMA((1,)),
+        ],
+        flops=6 * rows * width * width,
+        room=16,
+    )
     (out_msg,) = call(
-        functools.partial(attend, n_row, plan, rows, cols),
+        functools.partial(attend, rows),
         (shape((n_row, n_col, 2 * padded, LANES), bf16),),
-        [(a, "V") for a in parts + (w_key,)]
-        + [(a, "H") for a in (w_query, w_value, w_out, w_project)],
+        [(a, "V") for a in (others, x_own, k_own, by_head, own_seq, bias, wk)]
+        + [(a, "H") for a in (w_value, w_out, w_project)],
         [
             shape((width, width), bf16),
             shape((width, width), bf16),
-            shape((width, width), bf16),
             shape(w_project.shape, bf16),
-            shape((length, width), f32),
+            shape((rows, width), f32),
             shape((length, width), bf16),
             shape((length, width), bf16),
             shape((length, width), bf16),
-            shape((length, padded * HEADS), f32),
-            pltpu.SemaphoreType.DMA((4,)),
+            shape((padded * HEADS, length), f32),
+            shape((padded, width), bf16),
+            pltpu.SemaphoreType.DMA((3,)),
         ],
         flops=6 * length * width * width,
-        room=40,
+        room=32,
     )
     flat = out_msg.reshape(n_row * n_col, 2 * padded, LANES)
     got = lax.all_to_all(flat, ("row", "col"), split_axis=0, concat_axis=0, tiled=True)

time: 42.6 us -> 39.4 us (0.925)
  local copies, waits for them, and re-layouts: 1.6 us -> 0.01 us
  waiting for transfers between devices: 1.58 us -> 0.01 us
    unnamed x4 -> x2, local copies, waits for them, and re-layouts: 1.6 us -> 0.01 us
    ppermute x1, waiting for transfers between devices: 1.58 us -> 0.01 us  [local(): others = lax.ppermute(got, 'row', [(0, 1), (1, 0)])]
    pallas_call x3 -> x4, Pallas kernels: 9.55 us -> 9.44 us  [call(): pl.pallas_call(kernel, out_shape=outs, in_specs=[pl.BlockSpec(memory_spac...]
  transfers between devices with their start and end apart: 1 -> 1, of which waited for: 1 -> 0; matrix products, arithmetic and copies ran while one was open for 0% -> 0% of each run, Pallas kernels for 0% -> 6%
where the time goes in v2:
time: 39.4 us; the launch traced here: 39.2 us
  blocking collectives  29 us (74%)
  Pallas kernels  9.44 us (24%)
  between operations  0.67 us (2%)
    all_to_all x1, blocking collectives, local(): got = lax.all_to_all(msg, 'col', split_axis=0, concat_axis=0, tiled=True)  18.8 us
    all_to_all x1, blocking collectives, local(): lax.all_to_all(flat, ('row', 'col'), split_axis=0, concat_axis=0, tiled=T...  10.2 us
    pallas_call x4, Pallas kernels, call(): pl.pallas_call(kernel, out_shape=outs, in_specs=[pl.BlockSpec(memory_spac...  9.44 us
  transfers between devices with their start and end apart: 1, of which 0 were waited for; matrix products, arithmetic and copies ran while one was open for 0% of the time, Pallas kernels for 6%

profile of v2, /device:TPU:0, one launch (start us, length us, event | category | flops | bytes accessed | tf_op | source)
XLA Modules:
  0.0 39.2 jit_solution(15100542696239748090)
XLA Ops:
  0.6 3.0 %shard_map.122 = (bf16[12,96,128]{2,1,0:T(8,128)(2,1)S(1)}, bf16[16,72,128]{2,1,0:T(8,128)(2,1)S(1)}, bf16[1024,1024]{1,0:T(8,128)(2,1)S(1)}) custom-call(bf16[64,192]{1,0:T(8,128)(2,1)} %bitcast.10, bf16[128,512]{1,0:T(8,128)(2,1)} %refs_1_.1, bf16[512,128]{1,0:T(8,128)(2,1)} %refs_2_.1, bf16[32,128]{1,0:T(8,128)(2,1)} %bitcast.11, ...), custom_call_target="tpu_custom_call" | custom-call | flops 301989888 | bytes 5373952 | tf_op jit(solution)/shard_map/pallas_call | solution.py:47
  3.6 18.8 %all_to_all.10.got_ref = bf16[16,72,128]{2,1,0:T(8,128)(2,1)S(1)} all-to-all(bf16[16,72,128]{2,1,0:T(8,128)(2,1)S(1)} %get-tuple-element.12), channel_id=1, replica_groups=mesh['row'=2,'col'=16] {'col'}, dimensions={0} | all-to-all | bytes 589824 | tf_op jit(solution)/shard_map/all_to_all | solution.py:412
  22.4 0.0 collective-permute-start
  22.4 2.2 %shard_map.123 = (bf16[96,1024]{1,0:T(8,128)(2,1)S(1)}, bf16[96,1024]{1,0:T(8,128)(2,1)S(1)}, bf16[256,1024]{1,0:T(8,128)(2,1)S(1)}, f32[8,1024]{1,0:T(8,128)S(1)}, f32[192,256]{1,0:T(8,128)S(1)}) custom-call(bf16[16,72,128]{2,1,0:T(8,128)(2,1)S(1)} %all_to_all.10.got_ref, bf16[1024,1024]{1,0:T(8,128)(2,1)S(1)} %get-tuple-element.13.wk_ref, ...), custom_call_target="tpu_custom_call" | custom-call | flops 603979776 | bytes 5636096 | tf_op jit(solution)/shard_map/pallas_call | solution.py:47
  24.6 0.0 collective-permute-done.others_ref
  24.7 0.0 copy-start
  24.7 3.1 %shard_map.124 = bf16[2,16,16,128]{3,2,1,0:T(8,128)(2,1)S(1)} custom-call(bf16[16,72,128]{2,1,0:T(8,128)(2,1)S(1)} %collective-permute-done.others_ref, bf16[96,1024]{1,0:T(8,128)(2,1)S(1)} %get-tuple-element.14.x_own, bf16[96,1024]{1,0:T(8,128)(2,1)S(1)} %get-tuple-element.15.k_own, bf16[256,1024]{1,0:T(8,128)(2,1)S(1)} %get-tuple-element.16.by_head_ref, ...), custom_call_target="tpu_custom_call" | custom-call | flops 1207959552 | bytes 8126464 | tf_op jit(solution)/shard_map/pallas_call | solution.py:47
  27.8 10.2 %all_to_all.11 = bf16[32,16,128]{2,1,0:T(8,128)(2,1)S(1)} all-to-all(bf16[32,16,128]{2,1,0:T(8,128)(2,1)S(1)} %bitcast.7), channel_id=1, replica_groups=mesh['row'=2,'col'=16] {'row','col'}, dimensions={0} | all-to-all | bytes 262144 | tf_op jit(solution)/shard_map/all_to_all | solution.py:459
  38.0 0.0 copy-done
  38.0 1.1 %shard_map.125 = (bf16[12,96,128]{2,1,0:T(8,128)(2,1)}, bf16[64,96]{1,0:T(8,128)(2,1)}) custom-call(bf16[2,16,16,128]{3,2,1,0:T(8,128)(2,1)S(1)} %bitcast.8, bf16[12,96,128]{2,1,0:T(8,128)(2,1)S(1)} %get-tuple-element.19.mid_ref, bf16[128,128]{1,0:T(8,128)(2,1)S(1)} %copy-done), custom_call_target="tpu_custom_call" | custom-call | flops 37748736 | bytes 765952 | tf_op jit(solution)/shard_map/pallas_call | solution.py:47
Async XLA Ops:
  22.4 2.2 %collective-permute-start = (bf16[16,72,128]{2,1,0:T(8,128)(2,1)S(1)}, bf16[16,72,128]{2,1,0:T(8,128)(2,1)S(1)}, u32[]{:S(2)}, u32[]{:S(2)}) collective-permute-start(bf16[16,72,128]{2,1,0:T(8,128)(2,1)S(1)} %all_to_all.10.got_ref), channel_id=1, source_target_pairs={{0,16},{16,0},{1,17},{17,1},{2,18},{18,2},{3,19},{19,3},{4,20},{20... | collective-permute-start | bytes 884744 | tf_op jit(solution)/shard_map/ppermute | solution.py:414
  24.7 13.4 %copy-start = (bf16[128,128]{1,0:T(8,128)(2,1)S(1)}, bf16[128,128]{1,0:T(8,128)(2,1)}, u32[]{:S(2)}) copy-start(bf16[128,128]{1,0:T(8,128)(2,1)} %wpair_ref.1) | copy-start | bytes 98308

commit v3 on v2

--- a/solution.py
+++ b/solution.py
@@ -98,29 +98,31 @@
 
 
 def prepare(n_row, n_col, chunk, *refs):
-    mid_ref, msg_ref, wk_ref, seq_ref, hidden_ref, back_ref, bias_ref, pair_ref, norm_ref, sems = (
-        refs[6:]
-    )
-    wait = copies(refs[:6], (seq_ref, hidden_ref, back_ref, bias_ref, pair_ref, wk_ref), sems)
+    mid_ref, msg_ref, wq_ref, seq_ref, hidden_ref, back_ref, bias_ref, pair_ref = refs[6:14]
+    *inner_refs, sems = refs[14:]
+    wait = copies(refs[:6], (seq_ref, hidden_ref, back_ref, bias_ref, pair_ref, wq_ref), sems)
     cols, rows, chans = pair_ref.shape
     short = rows * seq_ref.shape[0] // LANES
     wait(0)
     pack_seq(n_row, rows, seq_ref, msg_ref)
     for k in range(1, 5):
         wait(k)
-    stage(lambda: transition(n_row, n_col, chunk, short, hidden_ref, back_ref, bias_ref, pair_ref, mid_ref, msg_ref, norm_ref))
+
+    @stage
+    def _():
+        weights = (hidden_ref, back_ref, bias_ref)
+        transition(n_col, chunk, short, *weights, pair_ref, mid_ref, msg_ref, *inner_refs)
+
     wait(5)
 
 
 def transition(
-    n_row, n_col, chunk, short, hidden_ref, back_ref, bias_ref, pair_ref, mid_ref, msg_ref, norm_ref
+    n_col, chunk, short,
+    hidden_ref, back_ref, bias_ref, pair_ref, mid_ref, msg_ref, norm_ref, full_ref, rest_ref,
 ):
     cols, rows, chans = pair_ref.shape
     own, keys, full, rest, split, _ = bias_plan(rows, cols, n_col)
     per_tile = LANES // HEADS
-    if keys > cols:
-        norm_ref[cols * rows :, :] = jnp.zeros(((keys - cols) * rows, chans), f32)
-
     def step(t):
         at = t * chunk
         pair = pair_ref[pl.ds(at, chunk)].reshape(chunk * rows, chans).astype(f32)
@@ -128,8 +130,8 @@
         hidden = jnp.maximum(dot(normed, hidden_ref[...]), 0.0).astype(bf16)
         mid = (pair + dot(hidden, back_ref[...])).astype(bf16)
         mid_ref[pl.ds(at, chunk)] = mid.reshape(chunk, rows, chans)
-        start = at * rows if isinstance(at, int) else pl.multiple_of(at * rows, 8)
-        norm_ref[pl.ds(start, chunk * rows), :] = layer_norm(mid.astype(f32))
+        normed = layer_norm(mid.astype(f32)).astype(bf16)
+        norm_ref[pl.ds(at, chunk)] = normed.reshape(chunk, rows, chans)
 
     if cols // chunk <= 4:
         for t in range(cols // chunk):
@@ -144,27 +146,39 @@
         for p in range(per_tile)
     ]
 
-    def queries(q):
-        parts = [norm_ref[pl.ds(c * own + q, keys, stride=rows), :] for c in range(n_col)]
-        return jnp.concatenate(parts, axis=0)
+    def queries(q, first, last):
+        some = norm_ref[first:last, q * n_col : (q + 1) * n_col, :]
+        return some.reshape((last - first) * n_col, chans)
+
+    def wide(qs, first, last):
+        return jnp.concatenate([queries(q, first, last) for q in qs], axis=1)
 
     for tile in range(full):
-        wide = jnp.concatenate(
-            [queries(tile * per_tile + p).astype(bf16) for p in range(per_tile)], axis=1
-        )
-        acc = dot_nt(wide, jnp.concatenate(placed, axis=1))
-        at = short + tile * keys
-        msg_ref[:, at : at + keys, :] = acc.reshape(n_col, keys, LANES).astype(bf16)
+        qs = range(tile * per_tile, (tile + 1) * per_tile)
+        acc = dot_nt(wide(qs, 0, cols), jnp.concatenate(placed, axis=1))
+        full_ref[tile, : cols * n_col, :] = acc
+        if keys > cols:
+            full_ref[tile, cols * n_col :, :] = jnp.zeros(((keys - cols) * n_col, LANES), f32)
+    small = keys // split
     if rest:
-        small = keys // split
-        lhs, rhs = [], []
-        for p in range(rest):
-            q_rows = queries(full * per_tile + p).reshape(n_col, split, small, chans)
-            for s in range(split):
-                lhs.append(q_rows[:, s].reshape(n_col * small, chans).astype(bf16))
-                rhs.append(placed[s * rest + p])
-        acc = dot_nt(jnp.concatenate(lhs, axis=1), jnp.concatenate(rhs, axis=1))
-        msg_ref[:, short + full * keys :, :] = acc.reshape(n_col, small, LANES).astype(bf16)
+        qs = range(full * per_tile, own)
+        for s in range(split):
+            first, last = s * small, min(cols, (s + 1) * small)
+            if last <= first:
+                continue
+            acc = dot_nt(
+                wide(qs, first, last),
+                jnp.concatenate(placed[s * rest : (s + 1) * rest], axis=1),
+            )
+            if s:
+                rest_ref[: (last - first) * n_col, :] += acc
+            else:
+                rest_ref[: (last - first) * n_col, :] = acc
+    for c in range(n_col):
+        parts = [full_ref[tile, pl.ds(c, keys, stride=n_col), :] for tile in range(full)]
+        if rest:
+            parts.append(rest_ref[pl.ds(c, small, stride=n_col), :])
+        msg_ref[c, short:, :] = jnp.concatenate(parts, axis=0).astype(bf16)
 
 
 def place(read, feats, short, x_ref, start):
@@ -185,11 +199,11 @@
 
 def own_block(
     plan, rows, cols,
-    got_ref, wk_ref, wq_hbm,
-    x_out, k_ref, by_head_ref, own_ref, bias_ref,
-    wq_ref, x_ref, raw_ref, norm_ref, sems,
+    got_ref, wq_ref, wk_hbm,
+    x_out, by_head_ref, own_ref, bias_ref, wk_ref,
+    x_ref, raw_ref, sems,
 ):
-    wait = copies((wq_hbm,), (wq_ref,), sems)
+    wait = copies((wk_hbm,), (wk_ref,), sems)
     own, keys, full, rest, split, _ = plan
     n_col = got_ref.shape[0]
     width = x_ref.shape[1]
@@ -203,10 +217,9 @@
         place(lambda c: got_ref[c, :short, :], feats, short, x_ref, 0)
         normed = layer_norm(x_ref[...]).astype(bf16)
         x_out[...] = normed
-        pick = one_hot_rows((padded, rows), lambda i: col * own + i)
+        pick = one_hot_rows((padded, rows), lambda i: i * n_col + col)
         own_ref[...] = dot(pick, x_ref[...].astype(bf16))
-        norm_ref[...] = dot(pick, normed).astype(bf16)
-        k_ref[...] = dot(normed, wk_ref[...]).astype(bf16)
+        own_norm = dot(pick, normed).astype(bf16)
 
         small = keys // split
         for c in range(n_col):
@@ -234,21 +247,19 @@
         same = (source == query * HEADS + target // padded) & (query < own)
         bias_ref[...] = dot(raw_ref[...].astype(bf16), same.astype(f32).astype(bf16))
 
-    wait(0)
-
-    @stage
-    def _():
-        queries = dot(norm_ref[...], wq_ref[...]).astype(bf16)
+        queries = dot(own_norm, wq_ref[...]).astype(bf16)
         spread = one_hot_rows((padded * HEADS, padded), lambda hi: hi % padded)
         wide = dot(spread, queries)
         head_of_row = lax.broadcasted_iota(jnp.int32, wide.shape, 0) // padded
         head_of_lane = lax.broadcasted_iota(jnp.int32, wide.shape, 1) // head_dim
         by_head_ref[...] = jnp.where(head_of_row == head_of_lane, wide, 0.0).astype(bf16)
 
+    wait(0)
+
 
 def attend(
     rows,
-    others_ref, x_own, k_own, by_head_ref, own_ref, bias_ref, wk_ref, wv_hbm, wo_hbm, wp_hbm,
+    others_ref, x_own, by_head_ref, own_ref, bias_ref, wk_ref, wv_hbm, wo_hbm, wp_hbm,
     out_ref,
     wv_ref, wo_ref, wp_ref, x_ref, xn_ref, k_ref, v_ref, w_ref, att_ref, sems,
 ):
@@ -268,7 +279,18 @@
         normed = layer_norm(x_ref[...]).astype(bf16)
         at = pl.ds(pl.multiple_of(v * rows, 16), rows)
         xn_ref[at, :] = normed
-        k_ref[at, :] = dot(normed, wk_ref[...]).astype(bf16)
+
+    step = rows * (2 if n_row == 2 else 1)
+
+    def project(w_of, out):
+        if length == step:
+            out[...] = dot(xn_ref[...], w_of[...]).astype(bf16)
+        else:
+
+            @pl.loop(0, length // step)
+            def _(b):
+                at = pl.ds(pl.multiple_of(b * step, 16), step)
+                out[at, :] = dot(xn_ref[at, :], w_of[...]).astype(bf16)
 
     @stage
     def _():
@@ -278,7 +300,7 @@
             pl.loop(0, n_row)(lambda v: block(lambda c: others_ref[v, c, :short, :], v))
         mine = pl.ds(pl.multiple_of(row * rows, 16), rows)
         xn_ref[mine, :] = x_own[...]
-        k_ref[mine, :] = k_own[...]
+        project(wk_ref, k_ref)
         scores = dot_nt(k_ref[...], by_head_ref[...]) * head_dim ** (-0.5) + bias_ref[...]
         top = jnp.max(scores, axis=0, keepdims=True)
         weights = jnp.exp(scores - top)
@@ -286,21 +308,12 @@
         w_ref[...] = (weights / denom).T
 
     wait(0)
-    step = rows * (2 if n_row == 2 else 1)
     per_group = LANES // head_dim
     tall = per_group * padded
 
     @stage
     def _():
-        if length == step:
-            v_ref[...] = dot(xn_ref[...], wv_ref[...]).astype(bf16)
-        else:
-
-            @pl.loop(0, length // step)
-            def _(b):
-                at = pl.ds(pl.multiple_of(b * step, 16), step)
-                v_ref[at, :] = dot(xn_ref[at, :], wv_ref[...]).astype(bf16)
-
+        project(wv_ref, v_ref)
         lane_head = lax.broadcasted_iota(jnp.int32, (padded, LANES), 1) // head_dim
         groups = []
         for g in range(width // LANES):
@@ -331,16 +344,30 @@
             )
 
 
-def update_pair(own, fold, msg_ref, mid_ref, wpair_ref, pair_ref, seq_ref, left_ref, slab_ref):
+def update_pair(
+    own, fold, chunk,
+    msg_ref, mid_ref, wpair_ref, pair_ref, seq_ref,
+    flat_ref, left_ref, right_ref, slab_ref,
+):
     cols, rows, chans = mid_ref.shape
     n_row, n_col, twice, _ = msg_ref.shape
-    padded = twice // 2
     half = chans // 2
     row, col = lax.axis_index("row"), lax.axis_index("col")
-    for c in range(n_col):
-        block = msg_ref[row, c].astype(f32)
-        left_ref[c * own : (c + 1) * own, :] = block[:own]
-        slab_ref[c * own : (c + 1) * own, :] = block[padded : padded + own]
+    flat_ref[...] = msg_ref[...].astype(f32).reshape(flat_ref.shape)
+    is_first = lax.broadcasted_iota(jnp.int32, (1, chans), 1) < half
+
+    def gathered(v, line):
+        return flat_ref[pl.ds(v * n_col * twice + line, n_col, stride=twice), :]
+
+    for q in range(own):
+        at = pl.ds(q * n_col, n_col)
+        left = gathered(row, q)
+        left_ref[at, :] = jnp.where(is_first, left, pltpu.roll(left, half, 1))
+        slab_ref[at, :] = gathered(row, twice // 2 + q)
+        for v in range(n_row):
+            right = gathered(v, q)
+            right = jnp.where(is_first, pltpu.roll(right, half, 1), right)
+            right_ref[pl.ds(v * rows + q * n_col, n_col), :] = right
     feats = LANES // fold
     turned = slab_ref[...].T
     for s in range(fold):
@@ -349,30 +376,23 @@
         def _():
             seq_ref[...] = turned[s * feats : (s + 1) * feats].astype(bf16)
 
-    both = left_ref[...]
-    is_first = lax.broadcasted_iota(jnp.int32, (1, chans), 1) < half
-    left = jnp.where(is_first, both, pltpu.roll(both, half, 1))
-    blocks_each = cols // own
-    first = col * blocks_each
+    left = left_ref[...]
 
     def step(t):
-        at = first + t
-        theirs = msg_ref[at // n_col, lax.rem(at, n_col)].astype(f32)[:padded]
-        right = jnp.where(is_first, pltpu.roll(theirs, half, 1), theirs)
         feature = []
-        for i in range(own):
-            r = right[i : i + 1]
-            feature.append(jnp.where(is_first, left * r, left - r).astype(bf16))
+        for j in range(chunk):
+            right = right_ref[pl.ds(col * cols + t * chunk + j, 1), :]
+            feature.append(jnp.where(is_first, left * right, left - right).astype(bf16))
         out = dot(jnp.concatenate(feature, axis=0), wpair_ref[...])
-        here = pl.ds(t * own, own)
+        here = pl.ds(t * chunk, chunk)
         mid = mid_ref[here].astype(f32)
-        pair_ref[here] = (mid + out.reshape(own, rows, chans)).astype(bf16)
-
-    if blocks_each <= 4:
-        for t in range(blocks_each):
+        pair_ref[here] = (mid + out.reshape(chunk, rows, chans)).astype(bf16)
+
+    if cols // chunk <= 4:
+        for t in range(cols // chunk):
             step(t)
     else:
-        pl.loop(0, blocks_each)(step)
+        pl.loop(0, cols // chunk)(step)
 
 
 def local(pair, seq, w_hidden, w_back, w_bias, w_query, w_key, w_value, w_out, w_project, w_pair):
@@ -389,21 +409,23 @@
     hidden_units = w_hidden.shape[1]
 
     chunk = max(k for k in range(1, cols + 1) if cols % k == 0 and k * rows <= 576)
-    pair_mid, msg, wk = call(
+    pair_mid, msg, wq = call(
         functools.partial(prepare, n_row, n_col, chunk),
         (
             shape((cols, rows, chans), bf16),
             shape((n_col, short + height, LANES), bf16),
             shape((width, width), bf16),
         ),
-        [(a, "H") for a in (seq.T, w_hidden, w_back, w_bias.T, pair.transpose(1, 0, 2), w_key)],
+        [(a, "H") for a in (seq.T, w_hidden, w_back, w_bias.T, pair.transpose(1, 0, 2), w_query)],
         [
             shape((feats, length), bf16),
             shape(w_hidden.shape, bf16),
             shape(w_back.shape, bf16),
             shape(w_bias.shape[::-1], bf16),
             shape((cols, rows, chans), bf16),
-            shape((keys * rows, chans), f32),
+            shape((cols, rows, chans), bf16),
+            shape((max(full, 1), keys * n_col, LANES), f32),
+            shape((keys * n_col, LANES), f32),
             pltpu.SemaphoreType.DMA((6,)),
         ],
         flops=4 * rows * cols * chans * hidden_units,
@@ -415,21 +437,19 @@
     else:
         others = lax.all_gather(got, "row")
     tiles = full + (1 if rest else 0)
-    x_own, k_own, by_head, own_seq, bias = call(
+    x_own, by_head, own_seq, bias, wk = call(
         functools.partial(own_block, plan, rows, cols),
         (
-            shape((rows, width), bf16),
             shape((rows, width), bf16),
             shape((padded * HEADS, width), bf16),
             shape((padded, width), f32),
             shape((length, padded * HEADS), f32),
+            shape((width, width), bf16),
         ),
-        [(got, "V"), (wk, "V"), (w_query, "H")],
+        [(got, "V"), (wq, "V"), (w_key, "H")],
         [
-            shape((width, width), bf16),
             shape((rows, width), f32),
             shape((length, tiles * LANES), f32),
-            shape((padded, width), bf16),
             pltpu.SemaphoreType.DMA((1,)),
         ],
         flops=6 * rows * width * width,
@@ -438,7 +458,7 @@
     (out_msg,) = call(
         functools.partial(attend, rows),
         (shape((n_row, n_col, 2 * padded, LANES), bf16),),
-        [(a, "V") for a in (others, x_own, k_own, by_head, own_seq, bias, wk)]
+        [(a, "V") for a in (others, x_own, by_head, own_seq, bias, wk)]
         + [(a, "H") for a in (w_value, w_out, w_project)],
         [
             shape((width, width), bf16),
@@ -458,13 +478,18 @@
     flat = out_msg.reshape(n_row * n_col, 2 * padded, LANES)
     got = lax.all_to_all(flat, ("row", "col"), split_axis=0, concat_axis=0, tiled=True)
     pair_out, seq_out = call(
-        functools.partial(update_pair, own, fold),
+        functools.partial(update_pair, own, fold, chunk),
         (
             jax.ShapeDtypeStruct((cols, rows, chans), bf16),
             jax.ShapeDtypeStruct((feats, rows), bf16),
         ),
         [(a, "V") for a in (got.reshape(out_msg.shape), pair_mid, w_pair)],
-        [pltpu.VMEM((rows, LANES), f32), pltpu.VMEM((rows, LANES), f32)],
+        [
+            shape((n_row * n_col * 2 * padded, LANES), f32),
+            shape((rows, LANES), f32),
+            shape((length, LANES), f32),
+            shape((rows, LANES), f32),
+        ],
         flops=2 * rows * cols * chans * chans,
     )
     return (pair_out.transpose(1, 0, 2), seq_out.T)

time: 39.4 us -> 38.5 us (0.977)
  Pallas kernels: 9.44 us -> 8.57 us
    pallas_call x4, Pallas kernels: 9.44 us -> 8.57 us  [call(): pl.pallas_call(kernel, out_shape=outs, in_specs=[pl.BlockSpec(memory_spac...]
  transfers between devices with their start and end apart: 1 -> 1, of which waited for: 0 -> 0; matrix products, arithmetic and copies ran while one was open for 0% -> 0% of each run, Pallas kernels for 6% -> 4%
where the time goes in v3:
time: 38.5 us; the launch traced here: 38.3 us
  blocking collectives  29 us (75%)
  Pallas kernels  8.57 us (22%)
  between operations  0.67 us (2%)
    all_to_all x1, blocking collectives, local(): got = lax.all_to_all(msg, 'col', split_axis=0, concat_axis=0, tiled=True)  18.8 us
    all_to_all x1, blocking collectives, local(): lax.all_to_all(flat, ('row', 'col'), split_axis=0, concat_axis=0, tiled=T...  10.2 us
    pallas_call x4, Pallas kernels, call(): pl.pallas_call(kernel, out_shape=outs, in_specs=[pl.BlockSpec(memory_spac...  8.57 us
  transfers between devices with their start and end apart: 1, of which 0 were waited for; matrix products, arithmetic and copies ran while one was open for 0% of the time, Pallas kernels for 4%

profile of v3, /device:TPU:0, one launch (start us, length us, event | category | flops | bytes accessed | tf_op | source)
XLA Modules:
  0.0 38.3 jit_solution(10301919832997393075)
XLA Ops:
  0.6 2.7 %shard_map.122 = (bf16[12,96,128]{2,1,0:T(8,128)(2,1)S(1)}, bf16[16,72,128]{2,1,0:T(8,128)(2,1)S(1)}, bf16[1024,1024]{1,0:T(8,128)(2,1)S(1)}) custom-call(bf16[64,192]{1,0:T(8,128)(2,1)} %bitcast.10, bf16[128,512]{1,0:T(8,128)(2,1)} %refs_1_.1, bf16[512,128]{1,0:T(8,128)(2,1)} %refs_2_.1, bf16[32,128]{1,0:T(8,128)(2,1)} %bitcast.11, ...), custom_call_target="tpu_custom_call" | custom-call | flops 301989888 | bytes 5373952 | tf_op jit(solution)/shard_map/pallas_call | solution.py:47
  3.4 18.8 %all_to_all.10.got_ref = bf16[16,72,128]{2,1,0:T(8,128)(2,1)S(1)} all-to-all(bf16[16,72,128]{2,1,0:T(8,128)(2,1)S(1)} %get-tuple-element.12), channel_id=1, replica_groups=mesh['row'=2,'col'=16] {'col'}, dimensions={0} | all-to-all | bytes 589824 | tf_op jit(solution)/shard_map/all_to_all | solution.py:434
  22.2 0.0 collective-permute-start
  22.2 1.6 %shard_map.123 = (bf16[96,1024]{1,0:T(8,128)(2,1)S(1)}, bf16[256,1024]{1,0:T(8,128)(2,1)S(1)}, f32[8,1024]{1,0:T(8,128)S(1)}, f32[192,256]{1,0:T(8,128)S(1)}, bf16[1024,1024]{1,0:T(8,128)(2,1)S(1)}) custom-call(bf16[16,72,128]{2,1,0:T(8,128)(2,1)S(1)} %all_to_all.10.got_ref, bf16[1024,1024]{1,0:T(8,128)(2,1)S(1)} %get-tuple-element.13.wq_ref, ...), custom_call_target="tpu_custom_call" | custom-call | flops 603979776 | bytes 7536640 | tf_op jit(solution)/shard_map/pallas_call | solution.py:47
  23.8 0.0 collective-permute-done.others_ref
  23.8 0.0 copy-start
  23.8 3.1 %shard_map.124 = bf16[2,16,16,128]{3,2,1,0:T(8,128)(2,1)S(1)} custom-call(bf16[16,72,128]{2,1,0:T(8,128)(2,1)S(1)} %collective-permute-done.others_ref, bf16[96,1024]{1,0:T(8,128)(2,1)S(1)} %get-tuple-element.14.x_own, bf16[256,1024]{1,0:T(8,128)(2,1)S(1)} %get-tuple-element.15.by_head_ref, f32[8,1024]{1,0:T(8,128)S(1)} %get-tuple-element.16.own_ref, ...), custom_call_target="tpu_custom_call" | custom-call | flops 1207959552 | bytes 7929856 | tf_op jit(solution)/shard_map/pallas_call | solution.py:47
  26.9 10.2 %all_to_all.11 = bf16[32,16,128]{2,1,0:T(8,128)(2,1)S(1)} all-to-all(bf16[32,16,128]{2,1,0:T(8,128)(2,1)S(1)} %bitcast.7), channel_id=1, replica_groups=mesh['row'=2,'col'=16] {'row','col'}, dimensions={0} | all-to-all | bytes 262144 | tf_op jit(solution)/shard_map/all_to_all | solution.py:479
  37.2 0.0 copy-done
  37.2 1.1 %shard_map.125 = (bf16[12,96,128]{2,1,0:T(8,128)(2,1)}, bf16[64,96]{1,0:T(8,128)(2,1)}) custom-call(bf16[2,16,16,128]{3,2,1,0:T(8,128)(2,1)S(1)} %bitcast.8, bf16[12,96,128]{2,1,0:T(8,128)(2,1)S(1)} %get-tuple-element.19.mid_ref, bf16[128,128]{1,0:T(8,128)(2,1)S(1)} %copy-done), custom_call_target="tpu_custom_call" | custom-call | flops 37748736 | bytes 765952 | tf_op jit(solution)/shard_map/pallas_call | solution.py:47
Async XLA Ops:
  22.2 1.6 %collective-permute-start = (bf16[16,72,128]{2,1,0:T(8,128)(2,1)S(1)}, bf16[16,72,128]{2,1,0:T(8,128)(2,1)S(1)}, u32[]{:S(2)}, u32[]{:S(2)}) collective-permute-start(bf16[16,72,128]{2,1,0:T(8,128)(2,1)S(1)} %all_to_all.10.got_ref), channel_id=1, source_target_pairs={{0,16},{16,0},{1,17},{17,1},{2,18},{18,2},{3,19},{19,3},{4,20},{20... | collective-permute-start | bytes 884744 | tf_op jit(solution)/shard_map/ppermute | solution.py:436
  23.8 13.4 %copy-start = (bf16[128,128]{1,0:T(8,128)(2,1)S(1)}, bf16[128,128]{1,0:T(8,128)(2,1)}, u32[]{:S(2)}) copy-start(bf16[128,128]{1,0:T(8,128)(2,1)} %wpair_ref.1) | copy-start | bytes 98308

commit v4 on v3

--- a/solution.py
+++ b/solution.py
@@ -68,61 +68,85 @@
     pl.when(lax.axis_index("row") >= 0)(body)
 
 
-def pack_seq(n_row, rows, seq_ref, msg_ref):
+GROUP = 4
+
+
+def folded(lines):
+    starts = range(0, lines.shape[0], GROUP)
+    return jnp.concatenate([lines[at : at + GROUP] for at in starts], axis=1)
+
+
+def lines_of(message, first, n):
+    tiles = range(first // GROUP, (first + n) // GROUP)
+    parts = [message(slice(t * LANES, (t + 1) * LANES)).astype(f32) for t in tiles]
+    return jnp.concatenate(parts, axis=0)
+
+
+def lanes_at(first, n):
+    return slice(first // GROUP * LANES, (first + n) // GROUP * LANES)
+
+
+def pack_seq(n_row, n_col, share, rows, seq_ref, msg_ref):
     feats = seq_ref.shape[0]
     fold = LANES // feats
-    short = rows // fold
+    short = rows // share // fold
     row = lax.axis_index("row")
+    turned = seq_ref[...].astype(f32).T
     for v in range(n_row):
 
         @pl.when(row == v)
         def _():
-            parts = [
-                seq_ref[:, v * rows + p * short : v * rows + (p + 1) * short].astype(f32)
-                for p in range(fold)
-            ]
-            tile = jnp.concatenate(parts, axis=0).T.astype(bf16)
-            msg_ref[:, :short, :] = jnp.broadcast_to(tile[None], (msg_ref.shape[0],) + tile.shape)
-
-
-def bias_plan(rows, cols, n_col):
-    own = rows // n_col
-    keys = round_up(cols, 16)
+            for u in range(share):
+                starts = range(v * rows + u * n_col, (v + 1) * rows, share * n_col)
+                some = jnp.concatenate([turned[at : at + n_col] for at in starts], axis=0)
+                tile = jnp.concatenate(
+                    [some[p * short : (p + 1) * short] for p in range(fold)], axis=1
+                )
+                tile = folded(tile).astype(bf16)
+                msg_ref[u * n_col : (u + 1) * n_col, :, lanes_at(0, short)] = jnp.broadcast_to(
+                    tile[None], (n_col,) + tile.shape
+                )
+
+
+def bias_plan(rows, cols, n_to):
+    own = rows // n_to
+    keys = round_up(cols, GROUP)
     per_tile = LANES // HEADS
     full, rest = divmod(own, per_tile)
     split = per_tile // rest if rest and per_tile % rest == 0 else 1
-    if rest and (keys // split) % 8:
+    if rest and keys % (8 * split):
         split = 1
     height = full * keys + (keys // split if rest else 0)
     return own, keys, full, rest, split, height
 
 
-def prepare(n_row, n_col, chunk, *refs):
+def prepare(n_row, n_col, share, chunk, *refs):
     mid_ref, msg_ref, wq_ref, seq_ref, hidden_ref, back_ref, bias_ref, pair_ref = refs[6:14]
     *inner_refs, sems = refs[14:]
     wait = copies(refs[:6], (seq_ref, hidden_ref, back_ref, bias_ref, pair_ref, wq_ref), sems)
     cols, rows, chans = pair_ref.shape
-    short = rows * seq_ref.shape[0] // LANES
+    short = rows // share * seq_ref.shape[0] // LANES
     wait(0)
-    pack_seq(n_row, rows, seq_ref, msg_ref)
+    pack_seq(n_row, n_col, share, rows, seq_ref, msg_ref)
     for k in range(1, 5):
         wait(k)
 
     @stage
     def _():
         weights = (hidden_ref, back_ref, bias_ref)
-        transition(n_col, chunk, short, *weights, pair_ref, mid_ref, msg_ref, *inner_refs)
+        transition(share * n_col, chunk, short, *weights, pair_ref, mid_ref, msg_ref, *inner_refs)
 
     wait(5)
 
 
 def transition(
-    n_col, chunk, short,
+    n_to, chunk, short,
     hidden_ref, back_ref, bias_ref, pair_ref, mid_ref, msg_ref, norm_ref, full_ref, rest_ref,
 ):
     cols, rows, chans = pair_ref.shape
-    own, keys, full, rest, split, _ = bias_plan(rows, cols, n_col)
+    own, keys, full, rest, split, height = bias_plan(rows, cols, n_to)
     per_tile = LANES // HEADS
+
     def step(t):
         at = t * chunk
         pair = pair_ref[pl.ds(at, chunk)].reshape(chunk * rows, chans).astype(f32)
@@ -147,8 +171,8 @@
     ]
 
     def queries(q, first, last):
-        some = norm_ref[first:last, q * n_col : (q + 1) * n_col, :]
-        return some.reshape((last - first) * n_col, chans)
+        some = norm_ref[first:last, q * n_to : (q + 1) * n_to, :]
+        return some.reshape((last - first) * n_to, chans)
 
     def wide(qs, first, last):
         return jnp.concatenate([queries(q, first, last) for q in qs], axis=1)
@@ -156,9 +180,9 @@
     for tile in range(full):
         qs = range(tile * per_tile, (tile + 1) * per_tile)
         acc = dot_nt(wide(qs, 0, cols), jnp.concatenate(placed, axis=1))
-        full_ref[tile, : cols * n_col, :] = acc
+        full_ref[tile, : cols * n_to, :] = acc
         if keys > cols:
-            full_ref[tile, cols * n_col :, :] = jnp.zeros(((keys - cols) * n_col, LANES), f32)
+            full_ref[tile, cols * n_to :, :] = jnp.zeros(((keys - cols) * n_to, LANES), f32)
     small = keys // split
     if rest:
         qs = range(full * per_tile, own)
@@ -171,21 +195,24 @@
                 jnp.concatenate(placed[s * rest : (s + 1) * rest], axis=1),
             )
             if s:
-                rest_ref[: (last - first) * n_col, :] += acc
+                rest_ref[: (last - first) * n_to, :] += acc
             else:
-                rest_ref[: (last - first) * n_col, :] = acc
-    for c in range(n_col):
-        parts = [full_ref[tile, pl.ds(c, keys, stride=n_col), :] for tile in range(full)]
+                rest_ref[: (last - first) * n_to, :] = acc
+                if last < small:
+                    rest_ref[last * n_to :, :] = jnp.zeros(((keys - last) * n_to, LANES), f32)
+    for c in range(n_to):
+        parts = [full_ref[tile, pl.ds(c, keys, stride=n_to), :] for tile in range(full)]
         if rest:
-            parts.append(rest_ref[pl.ds(c, small, stride=n_col), :])
-        msg_ref[c, short:, :] = jnp.concatenate(parts, axis=0).astype(bf16)
+            parts.append(rest_ref[pl.ds(c, small, stride=n_to), :])
+        lanes = lanes_at(short, height)
+        msg_ref[c, :, lanes] = jnp.concatenate([folded(p) for p in parts], axis=1).astype(bf16)
 
 
 def place(read, feats, short, x_ref, start):
     fold = LANES // feats
     slot = lax.broadcasted_iota(jnp.int32, (short, LANES), 1) // feats
     for g in range(x_ref.shape[1] // LANES):
-        got = [read(fold * g + s).astype(f32) for s in range(fold)]
+        got = [read(fold * g + s) for s in range(fold)]
         for p in range(fold):
             piece = got[p]
             for s in range(fold):
@@ -193,28 +220,33 @@
                     piece = jnp.where(
                         slot == s, pltpu.roll(got[s], (s - p) % fold * feats, 1), piece
                     )
-            at = pl.multiple_of(start + p * short, 16)
-            x_ref[pl.ds(at, short), g * LANES : (g + 1) * LANES] = piece
+            at = start + p * short
+            x_ref[at : at + short, g * LANES : (g + 1) * LANES] = piece
 
 
 def own_block(
-    plan, rows, cols,
+    plan, share, cols,
     got_ref, wq_ref, wk_hbm,
     x_out, by_head_ref, own_ref, bias_ref, wk_ref,
     x_ref, raw_ref, sems,
 ):
     wait = copies((wk_hbm,), (wk_ref,), sems)
     own, keys, full, rest, split, _ = plan
-    n_col = got_ref.shape[0]
-    width = x_ref.shape[1]
+    n_col = got_ref.shape[0] // share
+    rows, width = x_ref.shape
     feats = width // n_col
-    short = rows * feats // LANES
+    part = rows // share
+    short = part * feats // LANES
     head_dim = width // HEADS
     padded = own_ref.shape[0]
     col = lax.axis_index("col")
     @stage
     def _():
-        place(lambda c: got_ref[c, :short, :], feats, short, x_ref, 0)
+        for v in range(share):
+            place(
+                lambda c: lines_of(lambda at: got_ref[v * n_col + c, :, at], 0, short),
+                feats, short, x_ref, v * part,
+            )
         normed = layer_norm(x_ref[...]).astype(bf16)
         x_out[...] = normed
         pick = one_hot_rows((padded, rows), lambda i: i * n_col + col)
@@ -222,14 +254,16 @@
         own_norm = dot(pick, normed).astype(bf16)
 
         small = keys // split
-        for c in range(n_col):
+        tiles = raw_ref.shape[1] // share // LANES
+        for m in range(share * n_col):
+            c, lane = m % n_col, m // n_col * tiles * LANES
+            read = lambda at: got_ref[m, :, at]
             for tile in range(full):
-                at = short + tile * keys
-                raw_ref[c * cols : (c + 1) * cols, tile * LANES : (tile + 1) * LANES] = got_ref[
-                    c, at : at + keys, :
-                ].astype(f32)[:cols]
+                some = lines_of(read, short + tile * keys, keys)
+                raw_ref[c * cols : (c + 1) * cols, lane : lane + LANES] = some[:cols]
+                lane += LANES
             if rest:
-                last = got_ref[c, short + full * keys : short + full * keys + small, :].astype(f32)
+                last = lines_of(read, short + full * keys, small)
                 for s in range(split):
                     height = min(small, cols - s * small)
                     if height <= 0:
@@ -237,14 +271,14 @@
                     moved = last
                     if s:
                         moved = pltpu.roll(last, LANES - s * rest * HEADS, 1)
-                    raw_ref[c * cols + s * small : c * cols + s * small + height, full * LANES :] = (
-                        moved[:height]
-                    )
+                    at = c * cols + s * small
+                    raw_ref[at : at + height, lane : lane + LANES] = moved[:height]
         given = (raw_ref.shape[1], padded * HEADS)
         source = lax.broadcasted_iota(jnp.int32, given, 0)
         target = lax.broadcasted_iota(jnp.int32, given, 1)
         query = target % padded
-        same = (source == query * HEADS + target // padded) & (query < own)
+        lane = query // own * (tiles * LANES) + query % own * HEADS + target // padded
+        same = (source == lane) & (query < share * own)
         bias_ref[...] = dot(raw_ref[...].astype(bf16), same.astype(f32).astype(bf16))
 
         queries = dot(own_norm, wq_ref[...]).astype(bf16)
@@ -258,27 +292,34 @@
 
 
 def attend(
-    rows,
+    share, own, cols,
     others_ref, x_own, by_head_ref, own_ref, bias_ref, wk_ref, wv_hbm, wo_hbm, wp_hbm,
     out_ref,
     wv_ref, wo_ref, wp_ref, x_ref, xn_ref, k_ref, v_ref, w_ref, att_ref, sems,
 ):
     wait = copies((wv_hbm, wo_hbm, wp_hbm), (wv_ref, wo_ref, wp_ref), sems)
-    n_col = others_ref.shape[-3]
-    n_row = out_ref.shape[0]
+    n_row, n_col, lines, _ = out_ref.shape
     length, width = k_ref.shape
+    rows = x_ref.shape[0]
     feats = width // n_col
     fold = LANES // feats
-    short = rows // fold
+    part = rows // share
+    short = part // fold
     head_dim = width // HEADS
     padded = own_ref.shape[0]
     row = lax.axis_index("row")
 
+    def put(normed, v):
+        for k in range(rows // n_col):
+            at = k // own * rows + (k % own * share + v) * n_col
+            if share == 1:
+                at = v * rows + k * n_col
+            xn_ref[pl.ds(pl.multiple_of(at, 16), n_col), :] = normed[k * n_col : (k + 1) * n_col]
+
     def block(read, v):
-        place(read, feats, short, x_ref, 0)
-        normed = layer_norm(x_ref[...]).astype(bf16)
-        at = pl.ds(pl.multiple_of(v * rows, 16), rows)
-        xn_ref[at, :] = normed
+        for k in range(share):
+            place(lambda c: read(k * n_col + c), feats, short, x_ref, k * part)
+        put(layer_norm(x_ref[...]).astype(bf16), v)
 
     step = rows * (2 if n_row == 2 else 1)
 
@@ -294,12 +335,15 @@
 
     @stage
     def _():
-        if n_row == 2:
-            block(lambda c: others_ref[c, :short, :], 1 - row)
+        if share == 2:
+            block(lambda m: lines_of(lambda at: others_ref[m, :, at], 0, short), 1 - row)
         else:
-            pl.loop(0, n_row)(lambda v: block(lambda c: others_ref[v, c, :short, :], v))
-        mine = pl.ds(pl.multiple_of(row * rows, 16), rows)
-        xn_ref[mine, :] = x_own[...]
+
+            @pl.loop(0, n_row)
+            def _(v):
+                block(lambda m: lines_of(lambda at: others_ref[v, m, :, at], 0, short), v)
+
+        put(x_own[...], row)
         project(wk_ref, k_ref)
         scores = dot_nt(k_ref[...], by_head_ref[...]) * head_dim ** (-0.5) + bias_ref[...]
         top = jnp.max(scores, axis=0, keepdims=True)
@@ -337,37 +381,47 @@
         seq_next = (own_ref[...] + dot(att_ref[...], wo_ref[...])).astype(bf16)
         seq_wide = seq_next.astype(f32)
         projected = dot(layer_norm(seq_wide).astype(bf16), wp_ref[...]).astype(bf16).astype(f32)
-        for g in range(width // LANES):
-            tile = jnp.concatenate([projected, seq_wide[:, g * LANES : (g + 1) * LANES]], axis=0)
-            out_ref[:, fold * g : fold * (g + 1)] = jnp.broadcast_to(
-                tile.astype(bf16)[None, None], (n_row, fold) + tile.shape
-            )
+        is_left = lax.broadcasted_iota(jnp.int32, (own, LANES), 1) < LANES // 2
+        rest = jnp.zeros((lines - 2 * own, LANES), f32)
+        for v in range(n_row):
+            to = v * own if share == n_row else 0
+            for c in range(n_col):
+                of = c * cols // rows * own if share == n_row else 0
+                sides = jnp.where(
+                    is_left, projected[to : to + own], projected[of : of + own]
+                )
+                g = c // fold * LANES
+                slab = seq_wide[to : to + own, g : g + LANES]
+                out_ref[v, c] = jnp.concatenate([sides, slab, rest], axis=0).astype(bf16)
 
 
 def update_pair(
-    own, fold, chunk,
+    share, own, fold, chunk,
     msg_ref, mid_ref, wpair_ref, pair_ref, seq_ref,
     flat_ref, left_ref, right_ref, slab_ref,
 ):
     cols, rows, chans = mid_ref.shape
-    n_row, n_col, twice, _ = msg_ref.shape
+    n_row, n_col, lines, _ = msg_ref.shape
+    n_from = share * n_col
     half = chans // 2
     row, col = lax.axis_index("row"), lax.axis_index("col")
     flat_ref[...] = msg_ref[...].astype(f32).reshape(flat_ref.shape)
     is_first = lax.broadcasted_iota(jnp.int32, (1, chans), 1) < half
 
     def gathered(v, line):
-        return flat_ref[pl.ds(v * n_col * twice + line, n_col, stride=twice), :]
+        first = 0 if share == n_row else v * n_col * lines
+        return flat_ref[pl.ds(first + line, n_from, stride=lines), :]
 
     for q in range(own):
-        at = pl.ds(q * n_col, n_col)
+        at = pl.ds(q * n_from, n_from)
         left = gathered(row, q)
         left_ref[at, :] = jnp.where(is_first, left, pltpu.roll(left, half, 1))
-        slab_ref[at, :] = gathered(row, twice // 2 + q)
-        for v in range(n_row):
+        slab_ref[at, :] = gathered(row, own + q)
+        for v in range(right_ref.shape[0] // rows):
             right = gathered(v, q)
             right = jnp.where(is_first, pltpu.roll(right, half, 1), right)
-            right_ref[pl.ds(v * rows + q * n_col, n_col), :] = right
+            right_ref[pl.ds(v * rows + q * n_from, n_from), :] = right
+    first_key = lax.rem(col * cols, right_ref.shape[0])
     feats = LANES // fold
     turned = slab_ref[...].T
     for s in range(fold):
@@ -381,7 +435,7 @@
     def step(t):
         feature = []
         for j in range(chunk):
-            right = right_ref[pl.ds(col * cols + t * chunk + j, 1), :]
+            right = right_ref[pl.ds(first_key + t * chunk + j, 1), :]
             feature.append(jnp.where(is_first, left * right, left - right).astype(bf16))
         out = dot(jnp.concatenate(feature, axis=0), wpair_ref[...])
         here = pl.ds(t * chunk, chunk)
@@ -402,18 +456,22 @@
     width = w_query.shape[0]
     n_row, n_col = lax.axis_size("row"), lax.axis_size("col")
     fold = LANES // feats
-    short = rows // fold
-    plan = bias_plan(rows, cols, n_col)
+    share = 2 if n_row == 2 and rows % (2 * n_col) == 0 and rows % (16 * fold) == 0 else 1
+    n_to = share * n_col
+    everyone = ("row", "col") if share == n_row else "col"
+    short = rows // share // fold
+    plan = bias_plan(rows, cols, n_to)
     own, keys, full, rest, _, height = plan
-    padded = round_up(own, 8)
+    padded = round_up(share * own, 8)
+    lines = round_up(2 * own, 8)
     hidden_units = w_hidden.shape[1]
 
     chunk = max(k for k in range(1, cols + 1) if cols % k == 0 and k * rows <= 576)
     pair_mid, msg, wq = call(
-        functools.partial(prepare, n_row, n_col, chunk),
+        functools.partial(prepare, n_row, n_col, share, chunk),
         (
             shape((cols, rows, chans), bf16),
-            shape((n_col, short + height, LANES), bf16),
+            shape((n_to, GROUP, (short + height) // GROUP * LANES), bf16),
             shape((width, width), bf16),
         ),
         [(a, "H") for a in (seq.T, w_hidden, w_back, w_bias.T, pair.transpose(1, 0, 2), w_query)],
@@ -424,21 +482,21 @@
             shape(w_bias.shape[::-1], bf16),
             shape((cols, rows, chans), bf16),
             shape((cols, rows, chans), bf16),
-            shape((max(full, 1), keys * n_col, LANES), f32),
-            shape((keys * n_col, LANES), f32),
+            shape((max(full, 1), keys * n_to, LANES), f32),
+            shape((keys * n_to, LANES), f32),
             pltpu.SemaphoreType.DMA((6,)),
         ],
         flops=4 * rows * cols * chans * hidden_units,
         room=24,
     )
-    got = lax.all_to_all(msg, "col", split_axis=0, concat_axis=0, tiled=True)
-    if n_row == 2:
+    got = lax.all_to_all(msg, everyone, split_axis=0, concat_axis=0, tiled=True)
+    if share == 2:
         others = lax.ppermute(got, "row", [(0, 1), (1, 0)])
     else:
         others = lax.all_gather(got, "row")
     tiles = full + (1 if rest else 0)
     x_own, by_head, own_seq, bias, wk = call(
-        functools.partial(own_block, plan, rows, cols),
+        functools.partial(own_block, plan, share, cols),
         (
             shape((rows, width), bf16),
             shape((padded * HEADS, width), bf16),
@@ -449,15 +507,15 @@
         [(got, "V"), (wq, "V"), (w_key, "H")],
         [
             shape((rows, width), f32),
-            shape((length, tiles * LANES), f32),
+            shape((length, share * tiles * LANES), f32),
             pltpu.SemaphoreType.DMA((1,)),
         ],
         flops=6 * rows * width * width,
         room=16,
     )
     (out_msg,) = call(
-        functools.partial(attend, rows),
-        (shape((n_row, n_col, 2 * padded, LANES), bf16),),
+        functools.partial(attend, share, own, cols),
+        (shape((n_row, n_col, lines, LANES), bf16),),
         [(a, "V") for a in (others, x_own, by_head, own_seq, bias, wk)]
         + [(a, "H") for a in (w_value, w_out, w_project)],
         [
@@ -475,19 +533,19 @@
         flops=6 * length * width * width,
         room=32,
     )
-    flat = out_msg.reshape(n_row * n_col, 2 * padded, LANES)
+    flat = out_msg.reshape(n_row * n_col, lines, LANES)
     got = lax.all_to_all(flat, ("row", "col"), split_axis=0, concat_axis=0, tiled=True)
     pair_out, seq_out = call(
-        functools.partial(update_pair, own, fold, chunk),
+        functools.partial(update_pair, share, own, fold, chunk),
         (
             jax.ShapeDtypeStruct((cols, rows, chans), bf16),
             jax.ShapeDtypeStruct((feats, rows), bf16),
         ),
         [(a, "V") for a in (got.reshape(out_msg.shape), pair_mid, w_pair)],
         [
-            shape((n_row * n_col * 2 * padded, LANES), f32),
+            shape((n_row * n_col * lines, LANES), f32),
             shape((rows, LANES), f32),
-            shape((length, LANES), f32),
+            shape((rows if share == n_row else length, LANES), f32),
             shape((rows, LANES), f32),
         ],
         flops=2 * rows * cols * chans * chans,

time: 38.5 us -> 37.5 us (0.974)
  blocking collectives: 29 us -> 28 us
    all_to_all x1, blocking collectives: 10.2 us -> 9.02 us  [local(): lax.all_to_all(flat, ('row', 'col'), split_axis=0, concat_axis=0, tiled=T...]
where the time goes in v4:
time: 37.5 us; the launch traced here: 37.3 us
  blocking collectives  28 us (75%)
  Pallas kernels  8.57 us (23%)
  between operations  0.67 us (2%)
    all_to_all x1, blocking collectives, local(): got = lax.all_to_all(msg, everyone, split_axis=0, concat_axis=0, tiled=True)  19 us
    all_to_all x1, blocking collectives, local(): lax.all_to_all(flat, ('row', 'col'), split_axis=0, concat_axis=0, tiled=T...  9.02 us
    pallas_call x4, Pallas kernels, call(): pl.pallas_call(kernel, out_shape=outs, in_specs=[pl.BlockSpec(memory_spac...  8.57 us
  transfers between devices with their start and end apart: 1, of which 0 were waited for; matrix products, arithmetic and copies ran while one was open for 0% of the time, Pallas kernels for 4%

profile of v4, /device:TPU:0, one launch (start us, length us, event | category | flops | bytes accessed | tf_op | source)
XLA Modules:
  0.0 37.3 jit_solution(993225290702998569)
XLA Ops:
  0.6 2.8 %shard_map.122 = (bf16[12,96,128]{2,1,0:T(8,128)(2,1)S(1)}, bf16[32,4,1152]{2,1,0:T(4,128)(2,1)S(1)}, bf16[1024,1024]{1,0:T(8,128)(2,1)S(1)}) custom-call(bf16[64,192]{1,0:T(8,128)(2,1)} %bitcast.10, bf16[128,512]{1,0:T(8,128)(2,1)} %refs_1_.1, bf16[512,128]{1,0:T(8,128)(2,1)} %refs_2_.1, bf16[32,128]{1,0:T(8,128)(2,1)} %bitcast.11, ...), custom_call_target="tpu_custom_call" | custom-call | flops 301989888 | bytes 5373952 | tf_op jit(solution)/shard_map/pallas_call | solution.py:47
  3.4 19.0 %all_to_all.10.got_ref = bf16[32,4,1152]{2,1,0:T(4,128)(2,1)S(1)} all-to-all(bf16[32,4,1152]{2,1,0:T(4,128)(2,1)S(1)} %get-tuple-element.12), channel_id=1, replica_groups=mesh['row'=2,'col'=16] {'row','col'}, dimensions={0} | all-to-all | bytes 589824 | tf_op jit(solution)/shard_map/all_to_all | solution.py:492
  22.4 0.0 collective-permute-start
  22.4 1.6 %shard_map.123 = (bf16[96,1024]{1,0:T(8,128)(2,1)S(1)}, bf16[256,1024]{1,0:T(8,128)(2,1)S(1)}, f32[8,1024]{1,0:T(8,128)S(1)}, f32[192,256]{1,0:T(8,128)S(1)}, bf16[1024,1024]{1,0:T(8,128)(2,1)S(1)}) custom-call(bf16[32,4,1152]{2,1,0:T(4,128)(2,1)S(1)} %all_to_all.10.got_ref, bf16[1024,1024]{1,0:T(8,128)(2,1)S(1)} %get-tuple-element.13.wq_ref, ...), custom_call_target="tpu_custom_call" | custom-call | flops 603979776 | bytes 7536640 | tf_op jit(solution)/shard_map/pallas_call | solution.py:47
  24.0 0.0 collective-permute-done.others_ref
  24.0 0.0 copy-start
  24.0 3.1 %shard_map.124 = bf16[2,16,8,128]{3,2,1,0:T(8,128)(2,1)S(1)} custom-call(bf16[32,4,1152]{2,1,0:T(4,128)(2,1)S(1)} %collective-permute-done.others_ref, bf16[96,1024]{1,0:T(8,128)(2,1)S(1)} %get-tuple-element.14.x_own, bf16[256,1024]{1,0:T(8,128)(2,1)S(1)} %get-tuple-element.15.by_head_ref, f32[8,1024]{1,0:T(8,128)S(1)} %get-tuple-element.16.own_ref, ...), custom_call_target="tpu_custom_call" | custom-call | flops 1207959552 | bytes 7864320 | tf_op jit(solution)/shard_map/pallas_call | solution.py:47
  27.2 9.0 %all_to_all.11 = bf16[32,8,128]{2,1,0:T(8,128)(2,1)S(1)} all-to-all(bf16[32,8,128]{2,1,0:T(8,128)(2,1)S(1)} %bitcast.7), channel_id=1, replica_groups=mesh['row'=2,'col'=16] {'row','col'}, dimensions={0} | all-to-all | bytes 131072 | tf_op jit(solution)/shard_map/all_to_all | solution.py:537
  36.2 0.0 copy-done
  36.2 1.1 %shard_map.125 = (bf16[12,96,128]{2,1,0:T(8,128)(2,1)}, bf16[64,96]{1,0:T(8,128)(2,1)}) custom-call(bf16[2,16,8,128]{3,2,1,0:T(8,128)(2,1)S(1)} %bitcast.8, bf16[12,96,128]{2,1,0:T(8,128)(2,1)S(1)} %get-tuple-element.19.mid_ref, bf16[128,128]{1,0:T(8,128)(2,1)S(1)} %copy-done), custom_call_target="tpu_custom_call" | custom-call | flops 37748736 | bytes 700416 | tf_op jit(solution)/shard_map/pallas_call | solution.py:47
Async XLA Ops:
  22.4 1.6 %collective-permute-start = (bf16[32,4,1152]{2,1,0:T(4,128)(2,1)S(1)}, bf16[32,4,1152]{2,1,0:T(4,128)(2,1)S(1)}, u32[]{:S(2)}, u32[]{:S(2)}) collective-permute-start(bf16[32,4,1152]{2,1,0:T(4,128)(2,1)S(1)} %all_to_all.10.got_ref), channel_id=1, source_target_pairs={{0,16},{16,0},{1,17},{17,1},{2,18},{18,2},{3,19},{19,3},{4,20},{20... | collective-permute-start | bytes 884744 | tf_op jit(solution)/shard_map/ppermute | solution.py:494
  24.0 12.2 %copy-start = (bf16[128,128]{1,0:T(8,128)(2,1)S(1)}, bf16[128,128]{1,0:T(8,128)(2,1)}, u32[]{:S(2)}) copy-start(bf16[128,128]{1,0:T(8,128)(2,1)} %wpair_ref.1) | copy-start | bytes 98308

commit v5 on v4

--- a/solution.py
+++ b/solution.py
@@ -68,12 +68,12 @@
     pl.when(lax.axis_index("row") >= 0)(body)
 
 
-GROUP = 4
-
-
-def folded(lines):
-    starts = range(0, lines.shape[0], GROUP)
-    return jnp.concatenate([lines[at : at + GROUP] for at in starts], axis=1)
+GROUP = 2
+
+
+def folded(lines, group=GROUP):
+    starts = range(0, lines.shape[0], group)
+    return jnp.concatenate([lines[at : at + group] for at in starts], axis=1)
 
 
 def lines_of(message, first, n):
@@ -117,13 +117,21 @@
     if rest and keys % (8 * split):
         split = 1
     height = full * keys + (keys // split if rest else 0)
-    return own, keys, full, rest, split, height
+    base = 0
+    if full == 0 and rest == per_tile - 1 and cols % per_tile == 0:
+        base = cols // per_tile * rest
+        height = round_up(base, GROUP)
+    return own, keys, full, rest, split, height, base
 
 
 def prepare(n_row, n_col, share, chunk, *refs):
-    mid_ref, msg_ref, wq_ref, seq_ref, hidden_ref, back_ref, bias_ref, pair_ref = refs[6:14]
-    *inner_refs, sems = refs[14:]
-    wait = copies(refs[:6], (seq_ref, hidden_ref, back_ref, bias_ref, pair_ref, wq_ref), sems)
+    mid_ref, msg_ref, wq_ref, wva_ref, seq_ref, hidden_ref, back_ref, bias_ref, pair_ref = refs[7:16]
+    *inner_refs, sems = refs[16:]
+    wait = copies(
+        refs[:6] + (refs[6].at[:, pl.ds(0, wva_ref.shape[1])],),
+        (seq_ref, hidden_ref, back_ref, bias_ref, pair_ref, wq_ref, wva_ref),
+        sems,
+    )
     cols, rows, chans = pair_ref.shape
     short = rows // share * seq_ref.shape[0] // LANES
     wait(0)
@@ -137,6 +145,7 @@
         transition(share * n_col, chunk, short, *weights, pair_ref, mid_ref, msg_ref, *inner_refs)
 
     wait(5)
+    wait(6)
 
 
 def transition(
@@ -144,7 +153,7 @@
     hidden_ref, back_ref, bias_ref, pair_ref, mid_ref, msg_ref, norm_ref, full_ref, rest_ref,
 ):
     cols, rows, chans = pair_ref.shape
-    own, keys, full, rest, split, height = bias_plan(rows, cols, n_to)
+    own, keys, full, rest, split, height, base = bias_plan(rows, cols, n_to)
     per_tile = LANES // HEADS
 
     def step(t):
@@ -184,7 +193,18 @@
         if keys > cols:
             full_ref[tile, cols * n_to :, :] = jnp.zeros(((keys - cols) * n_to, LANES), f32)
     small = keys // split
-    if rest:
+    if base:
+        small = height
+        lines = [(base + m, q) for m in range(cols - base) for q in range(rest)]
+        sides = [queries(q, 0, base) for q in range(rest)]
+        sides.append(jnp.concatenate([queries(q, k, k + 1) for k, q in lines], axis=0))
+        acc = dot_nt(jnp.concatenate(sides, axis=1), jnp.concatenate(placed, axis=1))
+        rest_ref[: base * n_to, :] = acc
+        if height > base:
+            rest_ref[base * n_to : height * n_to, :] = jnp.zeros(
+                ((height - base) * n_to, LANES), f32
+            )
+    elif rest:
         qs = range(full * per_tile, own)
         for s in range(split):
             first, last = s * small, min(cols, (s + 1) * small)
@@ -226,12 +246,13 @@
 
 def own_block(
     plan, share, cols,
-    got_ref, wq_ref, wk_hbm,
-    x_out, by_head_ref, own_ref, bias_ref, wk_ref,
+    got_ref, wq_ref, wk_hbm, wv_hbm,
+    x_out, by_head_ref, own_ref, bias_ref, wk_ref, wvb_ref,
     x_ref, raw_ref, sems,
 ):
-    wait = copies((wk_hbm,), (wk_ref,), sems)
-    own, keys, full, rest, split, _ = plan
+    ahead = wvb_ref.shape[1]
+    wait = copies((wk_hbm, wv_hbm.at[:, pl.ds(ahead, ahead)]), (wk_ref, wvb_ref), sems)
+    own, keys, full, rest, split, height, base = plan
     n_col = got_ref.shape[0] // share
     rows, width = x_ref.shape
     feats = width // n_col
@@ -258,6 +279,10 @@
         for m in range(share * n_col):
             c, lane = m % n_col, m // n_col * tiles * LANES
             read = lambda at: got_ref[m, :, at]
+            if base:
+                some = lines_of(read, short, height)
+                raw_ref[c * base : (c + 1) * base, lane : lane + LANES] = some[:base]
+                continue
             for tile in range(full):
                 some = lines_of(read, short + tile * keys, keys)
                 raw_ref[c * cols : (c + 1) * cols, lane : lane + LANES] = some[:cols]
@@ -265,21 +290,41 @@
             if rest:
                 last = lines_of(read, short + full * keys, small)
                 for s in range(split):
-                    height = min(small, cols - s * small)
-                    if height <= 0:
+                    some = min(small, cols - s * small)
+                    if some <= 0:
                         continue
                     moved = last
                     if s:
                         moved = pltpu.roll(last, LANES - s * rest * HEADS, 1)
                     at = c * cols + s * small
-                    raw_ref[at : at + height, lane : lane + LANES] = moved[:height]
+                    raw_ref[at : at + some, lane : lane + LANES] = moved[:some]
         given = (raw_ref.shape[1], padded * HEADS)
         source = lax.broadcasted_iota(jnp.int32, given, 0)
         target = lax.broadcasted_iota(jnp.int32, given, 1)
         query = target % padded
         lane = query // own * (tiles * LANES) + query % own * HEADS + target // padded
         same = (source == lane) & (query < share * own)
-        bias_ref[...] = dot(raw_ref[...].astype(bf16), same.astype(f32).astype(bf16))
+        one_hot = lambda where: where.astype(f32).astype(bf16)
+        if base:
+            raw = raw_ref[: n_col * base, :].astype(bf16)
+            last = (query // own * LANES + rest * HEADS + target // padded == source) & (
+                query < share * own
+            )
+            early = dot(raw, one_hot(same)).astype(bf16)
+            late = dot(raw, one_hot(last)).astype(bf16)
+            which = (n_col * cols, n_col * base)
+            key = lax.broadcasted_iota(jnp.int32, which, 0)
+            line = lax.broadcasted_iota(jnp.int32, which, 1)
+            j = key % cols
+            begin = key // cols * base
+            total = dot(one_hot((j < base) & (line == begin + j)), early)
+            slot = lax.broadcasted_iota(jnp.int32, total.shape, 1) % padded % own
+            for q in range(own):
+                chosen = (j >= base) & (line == begin + (j - base) * own + q)
+                total = total + jnp.where(slot == q, dot(one_hot(chosen), late), 0.0)
+            bias_ref[...] = total
+        else:
+            bias_ref[...] = dot(raw_ref[...].astype(bf16), one_hot(same))
 
         queries = dot(own_norm, wq_ref[...]).astype(bf16)
         spread = one_hot_rows((padded * HEADS, padded), lambda hi: hi % padded)
@@ -289,16 +334,19 @@
         by_head_ref[...] = jnp.where(head_of_row == head_of_lane, wide, 0.0).astype(bf16)
 
     wait(0)
+    wait(1)
 
 
 def attend(
     share, own, cols,
-    others_ref, x_own, by_head_ref, own_ref, bias_ref, wk_ref, wv_hbm, wo_hbm, wp_hbm,
+    others_ref, x_own, by_head_ref, own_ref, bias_ref, wk_ref, wva_ref, wvb_ref, wv_hbm, wo_hbm, wp_hbm,
     out_ref,
     wv_ref, wo_ref, wp_ref, x_ref, xn_ref, k_ref, v_ref, w_ref, att_ref, sems,
 ):
-    wait = copies((wv_hbm, wo_hbm, wp_hbm), (wv_ref, wo_ref, wp_ref), sems)
-    n_row, n_col, lines, _ = out_ref.shape
+    ahead = wva_ref.shape[1]
+    last = wv_hbm.at[:, pl.ds(2 * ahead, wv_ref.shape[1])]
+    wait = copies((last, wo_hbm, wp_hbm), (wv_ref, wo_ref, wp_ref), sems)
+    n_row, n_col, pairs, _ = out_ref.shape
     length, width = k_ref.shape
     rows = x_ref.shape[0]
     feats = width // n_col
@@ -323,15 +371,16 @@
 
     step = rows * (2 if n_row == 2 else 1)
 
-    def project(w_of, out):
+    def project(w_of, out, first=0):
+        lanes = pl.ds(first, w_of.shape[1])
         if length == step:
-            out[...] = dot(xn_ref[...], w_of[...]).astype(bf16)
+            out[:, lanes] = dot(xn_ref[...], w_of[...]).astype(bf16)
         else:
 
             @pl.loop(0, length // step)
             def _(b):
                 at = pl.ds(pl.multiple_of(b * step, 16), step)
-                out[at, :] = dot(xn_ref[at, :], w_of[...]).astype(bf16)
+                out[at, lanes] = dot(xn_ref[at, :], w_of[...]).astype(bf16)
 
     @stage
     def _():
@@ -350,6 +399,8 @@
         weights = jnp.exp(scores - top)
         denom = jnp.sum(weights, axis=0, keepdims=True)
         w_ref[...] = (weights / denom).T
+        project(wva_ref, v_ref)
+        project(wvb_ref, v_ref, ahead)
 
     wait(0)
     per_group = LANES // head_dim
@@ -357,7 +408,7 @@
 
     @stage
     def _():
-        project(wv_ref, v_ref)
+        project(wv_ref, v_ref, 2 * ahead)
         lane_head = lax.broadcasted_iota(jnp.int32, (padded, LANES), 1) // head_dim
         groups = []
         for g in range(width // LANES):
@@ -382,7 +433,6 @@
         seq_wide = seq_next.astype(f32)
         projected = dot(layer_norm(seq_wide).astype(bf16), wp_ref[...]).astype(bf16).astype(f32)
         is_left = lax.broadcasted_iota(jnp.int32, (own, LANES), 1) < LANES // 2
-        rest = jnp.zeros((lines - 2 * own, LANES), f32)
         for v in range(n_row):
             to = v * own if share == n_row else 0
             for c in range(n_col):
@@ -392,7 +442,8 @@
                 )
                 g = c // fold * LANES
                 slab = seq_wide[to : to + own, g : g + LANES]
-                out_ref[v, c] = jnp.concatenate([sides, slab, rest], axis=0).astype(bf16)
+                tile = jnp.concatenate([sides, slab], axis=0)
+                out_ref[v, c] = folded(tile, pairs).astype(bf16)
 
 
 def update_pair(
@@ -401,16 +452,19 @@
     flat_ref, left_ref, right_ref, slab_ref,
 ):
     cols, rows, chans = mid_ref.shape
-    n_row, n_col, lines, _ = msg_ref.shape
+    n_row, n_col, pairs, _ = msg_ref.shape
     n_from = share * n_col
     half = chans // 2
     row, col = lax.axis_index("row"), lax.axis_index("col")
-    flat_ref[...] = msg_ref[...].astype(f32).reshape(flat_ref.shape)
+    for m in range(n_row * n_col):
+        message = msg_ref[m // n_col, m % n_col].astype(f32)
+        for t in range(own):
+            flat_ref[t, m * pairs : (m + 1) * pairs, :] = message[:, t * LANES : (t + 1) * LANES]
     is_first = lax.broadcasted_iota(jnp.int32, (1, chans), 1) < half
 
     def gathered(v, line):
-        first = 0 if share == n_row else v * n_col * lines
-        return flat_ref[pl.ds(first + line, n_from, stride=lines), :]
+        first = 0 if share == n_row else v * n_col * pairs
+        return flat_ref[line // pairs, pl.ds(first + line % pairs, n_from, stride=pairs), :]
 
     for q in range(own):
         at = pl.ds(q * n_from, n_from)
@@ -461,20 +515,25 @@
     everyone = ("row", "col") if share == n_row else "col"
     short = rows // share // fold
     plan = bias_plan(rows, cols, n_to)
-    own, keys, full, rest, _, height = plan
+    own, keys, full, rest, _, height, _ = plan
     padded = round_up(share * own, 8)
-    lines = round_up(2 * own, 8)
+    pairs, tiles_out = 2, own
     hidden_units = w_hidden.shape[1]
 
     chunk = max(k for k in range(1, cols + 1) if cols % k == 0 and k * rows <= 576)
-    pair_mid, msg, wq = call(
+    ahead = width // 4
+    pair_mid, msg, wq, wva = call(
         functools.partial(prepare, n_row, n_col, share, chunk),
         (
             shape((cols, rows, chans), bf16),
             shape((n_to, GROUP, (short + height) // GROUP * LANES), bf16),
             shape((width, width), bf16),
+            shape((width, ahead), bf16),
         ),
-        [(a, "H") for a in (seq.T, w_hidden, w_back, w_bias.T, pair.transpose(1, 0, 2), w_query)],
+        [
+            (a, "H")
+            for a in (seq.T, w_hidden, w_back, w_bias.T, pair.transpose(1, 0, 2), w_query, w_value)
+        ],
         [
             shape((feats, length), bf16),
             shape(w_hidden.shape, bf16),
@@ -484,7 +543,7 @@
             shape((cols, rows, chans), bf16),
             shape((max(full, 1), keys * n_to, LANES), f32),
             shape((keys * n_to, LANES), f32),
-            pltpu.SemaphoreType.DMA((6,)),
+            pltpu.SemaphoreType.DMA((7,)),
         ],
         flops=4 * rows * cols * chans * hidden_units,
         room=24,
@@ -495,7 +554,7 @@
     else:
         others = lax.all_gather(got, "row")
     tiles = full + (1 if rest else 0)
-    x_own, by_head, own_seq, bias, wk = call(
+    x_own, by_head, own_seq, bias, wk, wvb = call(
         functools.partial(own_block, plan, share, cols),
         (
             shape((rows, width), bf16),
@@ -503,23 +562,24 @@
             shape((padded, width), f32),
             shape((length, padded * HEADS), f32),
             shape((width, width), bf16),
+            shape((width, ahead), bf16),
         ),
-        [(got, "V"), (wq, "V"), (w_key, "H")],
+        [(got, "V"), (wq, "V"), (w_key, "H"), (w_value, "H")],
         [
             shape((rows, width), f32),
             shape((length, share * tiles * LANES), f32),
-            pltpu.SemaphoreType.DMA((1,)),
+            pltpu.SemaphoreType.DMA((2,)),
         ],
         flops=6 * rows * width * width,
         room=16,
     )
     (out_msg,) = call(
         functools.partial(attend, share, own, cols),
-        (shape((n_row, n_col, lines, LANES), bf16),),
-        [(a, "V") for a in (others, x_own, by_head, own_seq, bias, wk)]
+        (shape((n_row, n_col, pairs, tiles_out * LANES), bf16),),
+        [(a, "V") for a in (others, x_own, by_head, own_seq, bias, wk, wva, wvb)]
         + [(a, "H") for a in (w_value, w_out, w_project)],
         [
-            shape((width, width), bf16),
+            shape((width, width - 2 * ahead), bf16),
             shape((width, width), bf16),
             shape(w_project.shape, bf16),
             shape((rows, width), f32),
@@ -533,7 +593,7 @@
         flops=6 * length * width * width,
         room=32,
     )
-    flat = out_msg.reshape(n_row * n_col, lines, LANES)
+    flat = out_msg.reshape(n_row * n_col, pairs, tiles_out * LANES)
     got = lax.all_to_all(flat, ("row", "col"), split_axis=0, concat_axis=0, tiled=True)
     pair_out, seq_out = call(
         functools.partial(update_pair, share, own, fold, chunk),
@@ -543,7 +603,7 @@
         ),
         [(a, "V") for a in (got.reshape(out_msg.shape), pair_mid, w_pair)],
         [
-            shape((n_row * n_col * lines, LANES), f32),
+            shape((tiles_out, n_row * n_col * pairs, LANES), f32),
             shape((rows, LANES), f32),
             shape((rows if share == n_row else length, LANES), f32),
             shape((rows, LANES), f32),

time: 37.5 us -> 36.9 us (0.984)
  blocking collectives: 28 us -> 27.6 us
  transfers between devices with their start and end apart: 1 -> 1, of which waited for: 0 -> 0; matrix products, arithmetic and copies ran while one was open for 0% -> 0% of each run, Pallas kernels for 4% -> 5%
where the time goes in v5:
time: 36.9 us; the launch traced here: 36.7 us
  blocking collectives  27.6 us (75%)
  Pallas kernels  8.39 us (23%)
  between operations  0.67 us (2%)
    all_to_all x1, blocking collectives, local(): got = lax.all_to_all(msg, everyone, split_axis=0, concat_axis=0, tiled=True)  18.7 us
    all_to_all x1, blocking collectives, local(): lax.all_to_all(flat, ('row', 'col'), split_axis=0, concat_axis=0, tiled=T...  8.96 us
    pallas_call x4, Pallas kernels, call(): pl.pallas_call(kernel, out_shape=outs, in_specs=[pl.BlockSpec(memory_spac...  8.39 us
  transfers between devices with their start and end apart: 1, of which 0 were waited for; matrix products, arithmetic and copies ran while one was open for 0% of the time, Pallas kernels for 5%

profile of v5, /device:TPU:0, one launch (start us, length us, event | category | flops | bytes accessed | tf_op | source)
XLA Modules:
  0.0 36.7 jit_solution(11650361277169915906)
XLA Ops:
  0.6 2.8 %shard_map.122 = (bf16[12,96,128]{2,1,0:T(8,128)(2,1)S(1)}, bf16[32,2,2176]{2,1,0:T(2,128)(2,1)S(1)}, bf16[1024,1024]{1,0:T(8,128)(2,1)S(1)}, bf16[1024,256]{1,0:T(8,128)(2,1)S(1)}) custom-call(bf16[64,192]{1,0:T(8,128)(2,1)} %bitcast.10, bf16[128,512]{1,0:T(8,128)(2,1)} %refs_1_.1, bf16[512,128]{1,0:T(8,128)(2,1)} %refs_2_.1, bf16[32,128]{1,0:T(8,128)(2,1)} %bitcast.11, ...), custom_call_target="tpu_custom_call" | custom-call | flops 301989888 | bytes 7979008 | tf_op jit(solution)/shard_map/pallas_call | solution.py:47
  3.4 18.7 %all_to_all.10.got_ref = bf16[32,2,2176]{2,1,0:T(2,128)(2,1)S(1)} all-to-all(bf16[32,2,2176]{2,1,0:T(2,128)(2,1)S(1)} %get-tuple-element.14), channel_id=1, replica_groups=mesh['row'=2,'col'=16] {'row','col'}, dimensions={0} | all-to-all | bytes 557056 | tf_op jit(solution)/shard_map/all_to_all | solution.py:551
  22.1 0.0 collective-permute-start
  22.1 1.7 %shard_map.123 = (bf16[96,1024]{1,0:T(8,128)(2,1)S(1)}, bf16[256,1024]{1,0:T(8,128)(2,1)S(1)}, f32[8,1024]{1,0:T(8,128)S(1)}, f32[192,256]{1,0:T(8,128)S(1)}, bf...) custom-call(bf16[32,2,2176]{2,1,0:T(2,128)(2,1)S(1)} %all_to_all.10.got_ref, ...), custom_call_target="tpu_custom_call" | custom-call | flops 603979776 | bytes 10141696 | tf_op jit(solution)/shard_map/pallas_call | solution.py:47
  23.8 0.0 collective-permute-done.others_ref
  23.8 0.0 copy-start
  23.8 2.8 %shard_map.124 = bf16[2,16,2,384]{3,2,1,0:T(2,128)(2,1)S(1)} custom-call(bf16[32,2,2176]{2,1,0:T(2,128)(2,1)S(1)} %collective-permute-done.others_ref, bf16[96,1024]{1,0:T(8,128)(2,1)S(1)} %get-tuple-element.16.x_own, bf16[256,1024]{1,0:T(8,128)(2,1)S(1)} %get-tuple-element.17.by_head_ref, f32[8,1024]{1,0:T(8,128)S(1)} %get-tuple-element.18.own_ref, ...), custom_call_target="tpu_custom_call" | custom-call | flops 1207959552 | bytes 8880128 | tf_op jit(solution)/shard_map/pallas_call | solution.py:47
  26.6 9.0 %all_to_all.11 = bf16[32,2,384]{2,1,0:T(2,128)(2,1)S(1)} all-to-all(bf16[32,2,384]{2,1,0:T(2,128)(2,1)S(1)} %bitcast.7), channel_id=1, replica_groups=mesh['row'=2,'col'=16] {'row','col'}, dimensions={0} | all-to-all | bytes 98304 | tf_op jit(solution)/shard_map/all_to_all | solution.py:597
  35.6 0.0 copy-done
  35.6 1.1 %shard_map.125 = (bf16[12,96,128]{2,1,0:T(8,128)(2,1)}, bf16[64,96]{1,0:T(8,128)(2,1)}) custom-call(bf16[2,16,2,384]{3,2,1,0:T(2,128)(2,1)S(1)} %bitcast.8, bf16[12,96,128]{2,1,0:T(8,128)(2,1)S(1)} %get-tuple-element.23.mid_ref, bf16[128,128]{1,0:T(8,128)(2,1)S(1)} %copy-done), custom_call_target="tpu_custom_call" | custom-call | flops 37748736 | bytes 684032 | tf_op jit(solution)/shard_map/pallas_call | solution.py:47
Async XLA Ops:
  22.1 1.7 %collective-permute-start = (bf16[32,2,2176]{2,1,0:T(2,128)(2,1)S(1)}, bf16[32,2,2176]{2,1,0:T(2,128)(2,1)S(1)}, u32[]{:S(2)}, u32[]{:S(2)}) collective-permute-start(bf16[32,2,2176]{2,1,0:T(2,128)(2,1)S(1)} %all_to_all.10.got_ref), channel_id=1, source_target_pairs={{0,16},{16,0},{1,17},{17,1},{2,18},{18,2},{3,19},{19,3},{4,20},{20... | collective-permute-start | bytes 835592 | tf_op jit(solution)/shard_map/ppermute | solution.py:553
  23.8 11.8 %copy-start = (bf16[128,128]{1,0:T(8,128)(2,1)S(1)}, bf16[128,128]{1,0:T(8,128)(2,1)}, u32[]{:S(2)}) copy-start(bf16[128,128]{1,0:T(8,128)(2,1)} %wpair_ref.1) | copy-start | bytes 98308
